TPU v7x, 32 devices: a whole 2x2x4 slice. The times are simulated.
32 devices in a mesh: tier: 4 (over x, core), tile: 8 (over z, y).
Axes of the slice: x: 2, y: 2, z: 4, core: 2. Of those that a mesh axis runs over, the one named last changes fastest.
Arguments:
- starting_warmth_rise: float32 [32, 96, 1024], P('tile', 'tier'), may hold values from -3 to 8
- substance_per_cell: int32 [32, 96, 1024], P('tile', 'tier'), may hold values from 0 to 7
- material_transport_rates: float32 [2, 8], replicated, may hold values from 0.2 to 2
- patch_region_label: int32 [8, 8], P('tile'), may hold values from 0 to 15, as said below
- static_power_per_area: float32 [4, 16], replicated, may hold values from 0.5 to 4
- warming_power_factor: float32 [4, 16], replicated, may hold values from 0.2 to 0.8
- stacking_solve_operator: float32 [96, 96], replicated, may hold values from 0 to 1
Outputs:
- final_temperature: float32 [32, 96, 1024], P('tile', 'tier')
- block_power: float32 [4, 16], P('tier')
Inputs may be any that keep to these rules, and one draw needn't show every extreme that they name: `patch_region_label`: every block number names at least one tile.
All inputs are finite; a program needn't handle non-finite values.
Results may differ from a plain program's by a relative error of at most 0.0001.
Values sent between devices are 32-bit elements; how exact they have to be, the bound alone decides.
A program may use at most 64 MiB of HBM per device.

v0:
```python
import functools

import jax
import jax.numpy as jnp
from jax import lax
from jax.experimental import pallas as pl
from jax.experimental.pallas import tpu as pltpu
from jax.sharding import PartitionSpec as P

TILE_COLS = 128
LATERAL_RATE = 0.12
SOURCE_GAIN = 0.02
MESH = pl.DeviceIdType.MESH


def face(a, b):
    return (2.0 * LATERAL_RATE) * a * b / (a + b)


def solve(op, x):
    return jnp.dot(op, x, precision=lax.Precision.HIGHEST, preferred_element_type=jnp.float32)


def kernel(
    ntier, ntile, nblk,
    t_hbm, m_hbm, rates_hbm, labels_hbm, stat_hbm, fac_hbm, a_hbm,
    out, pw_out,
    t_in, m_in, rates, labels, stat, fac, a_in, s_in,
    halo_t, halo_m, mv, e_mat, e_mv, col_m, col_me, col_mh, col, col_e, t1, halo_1, mv2, res,
    cx, cy, cl, by_block, p1, p2a, p2b,
    s_halo, r_halo, s_a2a, r_a2a, s_mat, r_mat, s_me, r_me, s_e, r_e, s_out, r_out,
    s_p1, r_p1, s_pa, r_pa, s_pb, r_pb,
):
    tier = lax.axis_index("tier")
    tile = lax.axis_index("tile")
    rows, lev, width = t_in.shape
    cols = width // ntier
    quarter = cols // TILE_COLS
    levels = lev * ntier
    nmat = rates.shape[1]
    order = [r for r in range(1, rows - 1)] + [0, rows - 1]

    loads = [
        pltpu.make_async_copy(src, dst, s_in.at[i])
        for i, (src, dst) in enumerate(
            ((t_hbm, t_in), (m_hbm, m_in), (labels_hbm, labels), (rates_hbm, rates),
             (stat_hbm, stat), (fac_hbm, fac), (a_hbm, a_in))
        )
    ]
    for load in loads:
        load.start()

    def tier_at(k):
        return lax.rem(tier + k, ntier)

    def tile_at(k):
        return lax.rem(tile + k, ntile)

    def window(index):
        return pl.ds(pl.multiple_of(index * cols, TILE_COLS), cols)

    def group(index):
        return pl.ds(pl.multiple_of(index * lev, 8), lev)

    barrier = pltpu.get_barrier_semaphore()
    for k in range(1, ntier):
        pl.semaphore_signal(barrier, inc=1, device_id={"tier": tier_at(k)}, device_id_type=MESH)

    def greet(k, carry):
        pl.semaphore_signal(barrier, inc=1, device_id={"tile": tile_at(k)}, device_id_type=MESH)
        return carry

    lax.fori_loop(1, ntile, greet, 0)

    def lookup(codes, axes):
        outs = [jnp.full(codes.shape, rates[a, 0], jnp.float32) for a in axes]
        for m in range(1, nmat):
            hit = codes == m
            outs = [jnp.where(hit, rates[a, m], o) for a, o in zip(axes, outs)]
        return outs

    lane = lax.broadcasted_iota(jnp.int32, (lev, TILE_COLS), 1)
    pair = lane >> 1

    def pack_edges(src, dst):
        for d in range(ntier):
            low = max(d * cols - TILE_COLS, 0)
            high = min((d + 1) * cols, width - TILE_COLS)
            acc = jnp.zeros((lev, TILE_COLS), src.dtype)
            for r in range(rows):
                both = jnp.where(
                    lane == TILE_COLS - 1,
                    src[r, :, low : low + TILE_COLS],
                    src[r, :, high : high + TILE_COLS],
                )
                acc = jnp.where(pair == r, pltpu.roll(both, 2 * r + 1, 1), acc)
            dst[d] = acc

    blk1 = lax.broadcasted_iota(jnp.int32, (1, nblk), 1)
    blkn = lax.broadcasted_iota(jnp.int32, (ntier, nblk), 1)

    for load in loads:
        load.wait()
    sums = jnp.zeros((1, nblk), jnp.float32)
    areas = jnp.zeros((1, nblk), jnp.float32)
    active = t_in[0, 0:1, :]
    for r in range(1, rows):
        active = active + t_in[r, 0:1, :]
    for j in range(width // TILE_COLS):
        part = jnp.sum(active[:, j * TILE_COLS : (j + 1) * TILE_COLS], axis=1, keepdims=True)
        hit = blk1 == labels[0, j]
        sums = sums + jnp.where(hit, part, 0.0)
        areas = areas + jnp.where(hit, float(rows * TILE_COLS), 0.0)
    p1[0] = jnp.zeros(p1.shape[1:], jnp.float32)
    p1[0, 0:1, 0:nblk] = sums
    p1[0, 1:2, 0:nblk] = areas

    pl.semaphore_wait(barrier, ntier - 1 + ntile - 1)

    def share(buf, s_sem, r_sem):
        def send(k, carry):
            pltpu.make_async_remote_copy(
                src_ref=buf.at[0], dst_ref=buf.at[k], send_sem=s_sem, recv_sem=r_sem,
                device_id={"tile": tile_at(k)}, device_id_type=MESH,
            ).start()
            return carry

        lax.fori_loop(1, ntile, send, 0)

    def shared(buf, r_sem):
        rest = buf.at[pl.ds(1, ntile - 1)]
        pltpu.make_async_copy(rest, rest, r_sem).wait()

    def total(buf):
        return lax.fori_loop(1, ntile, lambda k, acc: acc + buf[k], buf[0])

    share(p1, s_p1, r_p1)

    def halo_copies(low_src, high_src, dst, which):
        down = pltpu.make_async_remote_copy(
            src_ref=low_src, dst_ref=dst.at[1],
            send_sem=s_halo.at[which, 0], recv_sem=r_halo.at[which, 1],
            device_id={"tile": lax.max(tile - 1, 0)}, device_id_type=MESH,
        )
        up = pltpu.make_async_remote_copy(
            src_ref=high_src, dst_ref=dst.at[0],
            send_sem=s_halo.at[which, 1], recv_sem=r_halo.at[which, 0],
            device_id={"tile": lax.min(tile + 1, ntile - 1)}, device_id_type=MESH,
        )
        return down, up

    has_low = tile > 0
    has_high = tile < ntile - 1

    def halo_start(copies):
        pl.when(has_low)(lambda: copies[0].start())
        pl.when(has_high)(lambda: copies[1].start())

    def halo_recv(copies):
        pl.when(has_low)(lambda: copies[1].wait_recv())
        pl.when(has_high)(lambda: copies[0].wait_recv())

    def halo_sent(copies):
        pl.when(has_low)(lambda: copies[0].wait_send())
        pl.when(has_high)(lambda: copies[1].wait_send())

    @pl.when(jnp.logical_not(has_low))
    def _():
        halo_t[0] = jnp.zeros(halo_t.shape[1:], jnp.float32)
        halo_m[0] = jnp.zeros(halo_m.shape[1:], jnp.int32)
        halo_1[0] = jnp.zeros(halo_1.shape[1:], jnp.float32)
        col_mh[0] = jnp.zeros(col_mh.shape[1:], jnp.int32)

    @pl.when(jnp.logical_not(has_high))
    def _():
        halo_t[1] = jnp.zeros(halo_t.shape[1:], jnp.float32)
        halo_m[1] = jnp.zeros(halo_m.shape[1:], jnp.int32)
        halo_1[1] = jnp.zeros(halo_1.shape[1:], jnp.float32)
        col_mh[1] = jnp.zeros(col_mh.shape[1:], jnp.int32)

    temp_halo = halo_copies(t_hbm.at[0], t_hbm.at[rows - 1], halo_t, 0)
    mat_halo = halo_copies(m_hbm.at[0], m_hbm.at[rows - 1], halo_m, 1)
    halo_start(temp_halo)
    halo_start(mat_halo)

    def to_tier(src, dst, s_sem, r_sem, k):
        return pltpu.make_async_remote_copy(
            src_ref=src, dst_ref=dst, send_sem=s_sem, recv_sem=r_sem,
            device_id={"tier": tier_at(k)}, device_id_type=MESH,
        )

    def mat_copy(k, receive):
        src = tier_at(ntier - k) if receive else tier
        return to_tier(
            m_hbm.at[:, :, window(tier_at(k))], col_m.at[:, group(src), :],
            s_mat.at[k], r_mat.at[k], k,
        )

    def edge_copy(k, receive, src_ref, dst_ref, s_sem, r_sem):
        src = tier_at(ntier - k) if receive else tier
        return to_tier(
            src_ref.at[tier_at(k)], dst_ref.at[group(src), :], s_sem.at[k], r_sem.at[k], k
        )

    def row_copy(r, k, receive):
        src = tier_at(ntier - k) if receive else tier
        return to_tier(
            mv.at[r, :, window(tier_at(k))], col.at[r, group(src), :],
            s_a2a.at[r, k], r_a2a.at[r, k], k,
        )

    def out_copy(r, k, receive):
        src = tier_at(ntier - k) if receive else tier
        return to_tier(
            res.at[r, group(tier_at(k)), :], out.at[r, :, window(src)],
            s_out.at[r, k], r_out.at[r, k], k,
        )

    for k in range(1, ntier):
        mat_copy(k, False).start()
    pack_edges(m_in, e_mat)
    for k in range(1, ntier):
        edge_copy(k, False, e_mat, col_me, s_me, r_me).start()
    col_m[:, group(tier), :] = m_in[:, :, window(tier)]
    col_me[group(tier), :] = e_mat[tier]

    wide = lax.broadcasted_iota(jnp.int32, (lev, width), 1)
    before = None
    for r in range(rows):
        kx, ky = lookup(m_in[r], (0, 1))
        here = t_in[r]
        flux = jnp.where(
            wide == width - 1, 0.0, face(ky, pltpu.roll(ky, width - 1, 1))
        ) * (pltpu.roll(here, width - 1, 1) - here)
        mv[r] = here + (flux - pltpu.roll(flux, 1, 1))
        if r > 0:
            flow = face(before, kx) * (here - t_in[r - 1])
            mv[r] -= flow
            mv[r - 1] += flow
        before = kx

    shared(p1, r_p1)
    whole = total(p1)
    count = whole[1:2, 0:nblk]
    power = stat[pl.ds(tier, 1), :] * jnp.exp(
        fac[pl.ds(tier, 1), :] * whole[0:1, 0:nblk] / count
    )
    gain = []
    for j in range(width // TILE_COLS):
        mine = jnp.sum(jnp.where(blk1 == labels[0, j], power, 0.0), axis=1, keepdims=True)
        gain.append(jnp.broadcast_to(SOURCE_GAIN * mine, (1, TILE_COLS)))
    gain = jnp.concatenate(gain, axis=1)
    for r in range(rows):
        mv[r, 0:1, :] += gain

    for r in order[:-2]:
        for k in range(1, ntier):
            row_copy(r, k, False).start()
        col[r, group(tier), :] = mv[r, :, window(tier)]

    halo_recv(temp_halo)
    halo_recv(mat_halo)
    for r, side, inside in ((0, 0, has_low), (rows - 1, 1, has_high)):
        (own,) = lookup(m_in[r], (0,))
        (other,) = lookup(halo_m[side], (0,))
        other = jnp.where(inside, other, 0.0)
        mv[r] += face(own, other) * (halo_t[side] - t_in[r])
        for k in range(1, ntier):
            row_copy(r, k, False).start()
        col[r, group(tier), :] = mv[r, :, window(tier)]
    pack_edges(mv, e_mv)
    for k in range(1, ntier):
        edge_copy(k, False, e_mv, col_e, s_e, r_e).start()
    col_e[group(tier), :] = e_mv[tier]

    level_sums = mv[0] + mv[1]
    for r in range(2, rows):
        level_sums = level_sums + mv[r]
    blkl = lax.broadcasted_iota(jnp.int32, (lev, nblk), 1)
    sums = jnp.zeros((lev, nblk), jnp.float32)
    for j in range(width // TILE_COLS):
        part = jnp.sum(
            level_sums[:, j * TILE_COLS : (j + 1) * TILE_COLS], axis=1, keepdims=True
        )
        sums = sums + jnp.where(blkl == labels[0, j], part, 0.0)
    by_block[...] = jnp.zeros_like(by_block)
    by_block[group(tier), :] = sums
    op = a_in[...]
    active_rows = jnp.concatenate(
        [op[t * lev : t * lev + 1, :] for t in range(ntier)]
        + [jnp.zeros((8 - ntier, levels), jnp.float32)],
        axis=0,
    )
    p2a[0] = jnp.zeros(p2a.shape[1:], jnp.float32)
    p2a[0, :, 0:nblk] = solve(active_rows, by_block[...])

    def tier_sum(k):
        return to_tier(p2a.at[0], p2a.at[k], s_pa.at[k], r_pa.at[k], k)

    for k in range(1, ntier):
        tier_sum(k).start()

    for k in range(1, ntier):
        mat_copy(k, True).wait_recv()
        edge_copy(k, True, e_mat, col_me, s_me, r_me).wait_recv()
    col_halo = halo_copies(col_m.at[0], col_m.at[rows - 1], col_mh, 2)
    halo_start(col_halo)
    narrow = lax.broadcasted_iota(jnp.int32, (levels, cols), 1)
    (ke,) = lookup(col_me[...], (1,))
    ke_low = jnp.where(tier > 0, ke, 0.0)
    ke_high = jnp.where(tier < ntier - 1, ke, 0.0)

    def at_first(edges, r):
        return pltpu.roll(edges, (TILE_COLS - 2 * r) % TILE_COLS, 1)

    def at_last(edges, r):
        return pltpu.roll(edges, TILE_COLS - 2 - 2 * r, 1)

    def widen(block):
        return jnp.concatenate([block] * quarter, axis=1)

    for r in range(rows):
        kx, ky = lookup(col_m[r], (0, 1))
        beside = jnp.where(
            narrow == cols - 1, widen(at_last(ke_high, r)), pltpu.roll(ky, cols - 1, 1)
        )
        cy[r] = face(ky, beside)
        cl[r] = face(ky[:, :TILE_COLS], at_first(ke_low, r))
        if r > 0:
            cx[r] = face(before, kx)
        before = kx
    for k in range(1, ntier):
        tier_sum(k).wait_recv()
    acc = p2a[0]
    for k in range(1, ntier):
        acc = acc + p2a[k]
    p2b[0] = acc
    share(p2b, s_pb, r_pb)

    for r in order:
        for k in range(1, ntier):
            row_copy(r, k, True).wait_recv()
        t1[r] = solve(op, col[r])
    one_halo = halo_copies(t1.at[0], t1.at[rows - 1], halo_1, 3)
    halo_start(one_halo)

    for k in range(1, ntier):
        edge_copy(k, True, e_mv, col_e, s_e, r_e).wait_recv()
    edges = solve(op, col_e[...])

    for r in range(rows):
        here = t1[r]
        beside = jnp.where(
            narrow == cols - 1, widen(at_last(edges, r)), pltpu.roll(here, cols - 1, 1)
        )
        flux = cy[r] * (beside - here)
        first = cl[r] * (here[:, :TILE_COLS] - at_first(edges, r))
        mv2[r] = here + (flux - jnp.where(narrow == 0, widen(first), pltpu.roll(flux, 1, 1)))
        if r > 0:
            flow = cx[r] * (here - t1[r - 1])
            mv2[r] -= flow
            mv2[r - 1] += flow

    shared(p2b, r_pb)
    whole = total(p2b)
    power = stat[...] * jnp.exp(fac[...] * whole[0:ntier, 0:nblk] / count)
    mine = lax.broadcasted_iota(jnp.int32, (ntier, nblk), 0) == tier
    pw_out[...] = jnp.sum(jnp.where(mine, power, 0.0), axis=0, keepdims=True)
    gain = []
    for q in range(quarter):
        hit = blkn == labels[0, tier * quarter + q]
        g = jnp.sum(jnp.where(hit, power, 0.0), axis=1, keepdims=True)
        gain.append(jnp.broadcast_to(SOURCE_GAIN * g, (ntier, TILE_COLS)))
    gain = jnp.concatenate(gain, axis=1)
    for r in range(rows):
        for t in range(ntier):
            mv2[r, t * lev : t * lev + 1, :] += gain[t : t + 1, :]

    def finish(r):
        res[r] = solve(op, mv2[r])
        for k in range(1, ntier):
            out_copy(r, k, False).start()
        out[r, :, window(tier)] = res[r, group(tier), :]

    for r in order[:-2]:
        finish(r)
    halo_recv(col_halo)
    for r, side, inside in ((0, 0, has_low), (rows - 1, 1, has_high)):
        (own,) = lookup(col_m[r], (0,))
        (other,) = lookup(col_mh[side], (0,))
        cx[r + side] = face(own, jnp.where(inside, other, 0.0))
    halo_recv(one_halo)
    for r, side in ((0, 0), (rows - 1, 1)):
        mv2[r] += cx[r + side] * (halo_1[side] - t1[r])
        finish(r)

    for r in order:
        for k in range(1, ntier):
            out_copy(r, k, True).wait_recv()

    for copies in (temp_halo, mat_halo, col_halo, one_halo):
        halo_sent(copies)
    for k in range(1, ntier):
        mat_copy(k, False).wait_send()
        edge_copy(k, False, e_mat, col_me, s_me, r_me).wait_send()
        edge_copy(k, False, e_mv, col_e, s_e, r_e).wait_send()
        tier_sum(k).wait_send()
        for r in range(rows):
            row_copy(r, k, False).wait_send()
            out_copy(r, k, False).wait_send()
    shared(p1, s_p1)
    shared(p2b, s_pb)


def solution(mesh):
    ntier, ntile = mesh.shape["tier"], mesh.shape["tile"]

    def shards(temp, mats, rates, labels, stat, fac, op):
        rows, lev, width = temp.shape
        nblk = stat.shape[1]
        pad = -(-nblk // 128) * 128
        cols, levels = width // ntier, lev * ntier
        f32, i32 = jnp.float32, jnp.int32
        vm = lambda shape, dtype=f32: pltpu.VMEM(shape, dtype)
        dma = pltpu.SemaphoreType.DMA
        vmem = pl.BlockSpec(memory_space=pltpu.VMEM)
        return pl.pallas_call(
            functools.partial(kernel, ntier, ntile, nblk),
            out_shape=(
                jax.ShapeDtypeStruct(temp.shape, f32),
                jax.ShapeDtypeStruct((1, nblk), f32),
            ),
            in_specs=[pl.BlockSpec(memory_space=pltpu.HBM)] * 7,
            out_specs=(vmem, vmem),
            scratch_shapes=[
                vm(temp.shape), vm(mats.shape, i32), pltpu.SMEM(rates.shape, f32),
                pltpu.SMEM(labels.shape, i32), vm(stat.shape), vm(fac.shape), vm(op.shape),
                dma((7,)),
                vm((2, lev, width)), vm((2, lev, width), i32), vm((rows, lev, width)),
                vm((ntier, lev, TILE_COLS), i32), vm((ntier, lev, TILE_COLS)),
                vm((rows, levels, cols), i32), vm((levels, TILE_COLS), i32),
                vm((2, levels, cols), i32),
                vm((rows, levels, cols)), vm((levels, TILE_COLS)), vm((rows, levels, cols)),
                vm((2, levels, cols)), vm((rows, levels, cols)), vm((rows, levels, cols)),
                vm((rows + 1, levels, cols)), vm((rows, levels, cols)),
                vm((rows, levels, TILE_COLS)),
                vm((levels, nblk)), vm((ntile, 8, pad)), vm((ntier, 8, pad)), vm((ntile, 8, pad)),
                dma((4, 2)), dma((4, 2)), dma((rows, ntier)), dma((rows, ntier)),
                dma((ntier,)), dma((ntier,)), dma((ntier,)), dma((ntier,)),
                dma((ntier,)), dma((ntier,)), dma((rows, ntier)), dma((rows, ntier)),
                dma, dma, dma((ntier,)), dma((ntier,)), dma, dma,
            ],
            compiler_params=pltpu.CompilerParams(
                collective_id=0, has_side_effects=True, vmem_limit_bytes=62 * 1024 * 1024
            ),
        )(temp, mats, rates, labels, stat, fac, op)

    return jax.shard_map(
        shards,
        mesh=mesh,
        in_specs=(P("tile", "tier", None), P("tile", "tier", None), P(), P("tile", None), P(), P(), P()),
        out_specs=(P("tile", "tier", None), P("tier", None)),
        check_vma=False,
    )
```

profile of v0, /device:TPU:0, one launch (start us, length us, event | category | flops | bytes accessed | tf_op | source)
XLA Modules:
  0.0 35.0 jit_solution(15889908747206125200)
XLA Ops:
  0.6 32.1 %shard_map.86 = (f32[4,24,1024]{2,1,0:T(8,128)}, f32[1,16]{1,0:T(1,128)}) custom-call(f32[4,24,1024]{2,1,0:T(8,128)} %t_hbm.1, s32[4,24,1024]{2,1,0:T(8,128)} %m_hbm.1, f32[2,8]{1,0:T(2,128)} %rates_hbm.1, s32[1,8]{1,0:T(1,128)} %labels_hbm.1, f32[4,16]{1,0:T(4,128)} %stat_hbm.1, f32[4,16]{1,0:T(4,128)} %fac_hbm.1, f32[96,96]{1,0:T(8,128)} %a_hbm.1), custom_call_target="tpu_custom_call" | custom-call | tf_op jit(solution)/shard_map/pallas_call | solution.py:427
  32.7 0.0 copy-start
  32.7 1.8 %copy.11 = f32[4,24,1024]{2,1,0:T(8,128)} copy(f32[4,24,1024]{2,1,0:T(8,128)} %get-tuple-element.4) | data formatting | bytes 786432
  34.5 0.0 copy-done
  34.5 0.5 %copy.12 = f32[1,16]{1,0:T(1,128)} copy(f32[1,16]{1,0:T(1,128)S(1)} %copy-done) | data formatting | bytes 128
Async XLA Ops:
  32.7 1.8 %copy-start = (f32[1,16]{1,0:T(1,128)S(1)}, f32[1,16]{1,0:T(1,128)}, u32[]{:S(2)}) copy-start(f32[1,16]{1,0:T(1,128)} %get-tuple-element.5) | copy-start | bytes 196
where the time goes:
time: 35.2 us; the launch traced here: 35 us
  Pallas kernels  32.1 us (91%)
  local copies, waits for them, and re-layouts  2.28 us (6%)
  between operations  0.65 us (2%)
    pallas_call x1, Pallas kernels, shards(): pl.pallas_call(functools.partial(kernel, ntier, ntile, nblk), out_shape=(...  32.1 us
    unnamed x4, local copies, waits for them, and re-layouts  2.28 us

commit v1 on v0

v1 whole, which is shorter than its diff:
```python
import functools

import jax
import jax.numpy as jnp
from jax import lax
from jax.experimental import pallas as pl
from jax.experimental.pallas import tpu as pltpu
from jax.sharding import PartitionSpec as P

C = 128
RATE = 0.12
SOURCE_GAIN = 0.02
MESH = pl.DeviceIdType.MESH


def solve(op, x):
    return jnp.dot(op, x, precision=lax.Precision.HIGHEST, preferred_element_type=jnp.float32)


def roll(x, shift):
    return pltpu.roll(x, shift % C, x.ndim - 1) if shift % C else x


def kernel(
    ntier, ntile, nblk, group,
    t_hbm, m_hbm, rates_hbm, labels_hbm, stat_hbm, fac_hbm, a_hbm,
    out, pw_out,
    t_in, m_in, rates, labels, stat, fac, a_in, s_in,
    col_t, col_m, halo_t, halo_m, halo_1,
    pk_out, pk, halo_p,
    cx, cy, ce, mv, t1, t1c, res,
    p1g, p1z, p2g, p2z,
    s_t, s_m, s_pk, s_o,
    r_et, r_em, r_rt, r_rm, r_pk, r_o,
    s_h, r_h,
    s_p1g, r_p1g, s_p1z, r_p1z, s_p2g, r_p2g, s_p2z, r_p2z,
):
    tier = lax.axis_index("tier")
    tile = lax.axis_index("tile")
    rows, lev, width = t_in.shape
    levels = lev * ntier
    nmat = rates.shape[1]
    ngrp = ntile // group
    grows = rows * group
    sub = lax.rem(tile, group)
    base = tile - sub
    place = tile // group
    own = tier * group + sub
    nwin = ntier * group
    active_rows = [t * lev for t in range(ntier)]

    loads = [
        pltpu.make_async_copy(src, dst, s_in.at[i])
        for i, (src, dst) in enumerate(
            ((t_hbm, t_in), (m_hbm, m_in), (labels_hbm, labels), (rates_hbm, rates),
             (stat_hbm, stat), (fac_hbm, fac), (a_hbm, a_in))
        )
    ]
    for load in loads:
        load.start()

    peers = []
    for a in range(ntier):
        for b in range(group):
            t2 = lax.rem(tier + a, ntier)
            s2 = lax.rem(sub + b, group)
            peers.append((a == 0 and b == 0, t2, s2))

    def there(t2, s2):
        return {"tier": t2, "tile": base + s2}

    barrier = pltpu.get_barrier_semaphore()
    for mine, t2, s2 in peers:
        if not mine:
            pl.semaphore_signal(barrier, inc=1, device_id=there(t2, s2), device_id_type=MESH)

    def across(k):
        return {"tile": lax.rem(tile + k * group, ntile)}

    def greet(k, carry):
        pl.semaphore_signal(barrier, inc=1, device_id=across(k), device_id_type=MESH)
        return carry

    lax.fori_loop(1, ngrp, greet, 0)

    def cols(w):
        return pl.ds(pl.multiple_of(w * C, C), C)

    def levs(t):
        return pl.ds(pl.multiple_of(t * lev, 8), lev)

    lane = lax.broadcasted_iota(jnp.int32, (1, C), 1)
    blk = lax.broadcasted_iota(jnp.int32, (1, nblk), 1)

    for load in loads:
        load.wait()

    sums = jnp.zeros((1, nblk), jnp.float32)
    areas = jnp.zeros((1, nblk), jnp.float32)
    names = jnp.zeros((1, C), jnp.float32)
    active = t_in[0, 0:1, :]
    for r in range(1, rows):
        active = active + t_in[r, 0:1, :]
    for j in range(width // C):
        part = jnp.sum(active[:, j * C : (j + 1) * C], axis=1, keepdims=True)
        hit = blk == labels[0, j]
        sums = sums + jnp.where(hit, part, 0.0)
        areas = areas + jnp.where(hit, float(rows * C), 0.0)
        names = jnp.where(lane == j, labels[0, j].astype(jnp.float32), names)
    p1g[own] = jnp.zeros(p1g.shape[1:], jnp.float32)
    p1g[own, 0:1, 0:nblk] = sums
    p1g[own, 1:2, 0:nblk] = areas
    p1g[own, 2:3, 0:C] = names

    pl.semaphore_wait(barrier, nwin - 1 + ngrp - 1)

    def group_send(buf, s_sem, r_sem):
        for mine, t2, s2 in peers:
            if not mine:
                pltpu.make_async_remote_copy(
                    src_ref=buf.at[own], dst_ref=buf.at[own], send_sem=s_sem, recv_sem=r_sem,
                    device_id=there(t2, s2), device_id_type=MESH,
                ).start()

    def across_send(buf, s_sem, r_sem):
        def send(k, carry):
            pltpu.make_async_remote_copy(
                src_ref=buf.at[0], dst_ref=buf.at[k], send_sem=s_sem, recv_sem=r_sem,
                device_id=across(k), device_id_type=MESH,
            ).start()
            return carry

        lax.fori_loop(1, ngrp, send, 0)

    def wait_for(ref, sem):
        pltpu.make_async_copy(ref, ref, sem).wait()

    def all_but_one(buf, sem):
        wait_for(buf.at[pl.ds(1, buf.shape[0] - 1)], sem)

    def total(buf):
        return lax.fori_loop(1, ngrp, lambda k, acc: acc + buf[k], buf[0])

    group_send(p1g, s_p1g, r_p1g)

    def spread(src, dst, row, to, count, s_sem, r_sem):
        for mine, t2, s2 in peers:
            src_ref = src.at[pl.ds(row, count), :, cols(t2 * group + s2)]
            dst_ref = dst.at[pl.ds(to, count), levs(tier), :]
            if mine:
                pltpu.make_async_copy(src_ref, dst_ref, r_sem).start()
            else:
                pltpu.make_async_remote_copy(
                    src_ref=src_ref, dst_ref=dst_ref, send_sem=s_sem, recv_sem=r_sem,
                    device_id=there(t2, s2), device_id_type=MESH,
                ).start()

    edge = lax.select(sub == 0, 0, rows - 1)
    rest = lax.select(sub == 0, 1, 0)
    spread(t_hbm, col_t, edge, sub * rows + edge, 1, s_t, r_et.at[sub])
    spread(m_hbm, col_m, edge, sub * rows + edge, 1, s_m, r_em.at[sub])

    quad = lane >> 2
    for w in range(nwin):
        low = max(w - 1, 0) * C
        high = min(w + 1, nwin - 1) * C
        for g in range(lev // 8):
            ls = slice(8 * g, 8 * g + 8)
            acc = None
            for q, src in ((0, t_in), (rows, m_in)):
                for r in range(rows):
                    both = jnp.where(
                        lane >= 64, src[r, ls, low : low + C], src[r, ls, high : high + C]
                    )
                    if q:
                        both = both.astype(jnp.float32)
                    put = roll(both, 32 * g + 4 * (q + r) + 2)
                    acc = put if acc is None else jnp.where(quad == 8 * g + q + r, put, acc)
            pk_out[w, g] = acc

    def fold(w):
        total_p = None
        for g in range(lev // 8):
            piece = pk_out[w, g]
            keep = (lane >= 32 * g) & (lane < 32 * g + 32)
            total_p = jnp.where(keep, piece, 0.0) if total_p is None else jnp.where(keep, piece, total_p)
        return total_p

    for w in range(nwin):
        pk_out[w, 0] = fold(w)

    for mine, t2, s2 in peers:
        src_ref, dst_ref = pk_out.at[t2 * group + s2, 0], pk.at[sub, tier]
        if mine:
            pltpu.make_async_copy(src_ref, dst_ref, r_pk).start()
        else:
            pltpu.make_async_remote_copy(
                src_ref=src_ref, dst_ref=dst_ref, send_sem=s_pk, recv_sem=r_pk,
                device_id=there(t2, s2), device_id_type=MESH,
            ).start()
    spread(m_hbm, col_m, rest, sub * rows + rest, rows - 1, s_m, r_rm)
    spread(t_hbm, col_t, rest, sub * rows + rest, rows - 1, s_t, r_rt)

    has_low = place > 0
    has_high = place < ngrp - 1

    @pl.when(jnp.logical_not(has_low))
    def _():
        for ref in (halo_t, halo_m, halo_p, halo_1):
            ref[0] = jnp.zeros(ref.shape[1:], ref.dtype)

    @pl.when(jnp.logical_not(has_high))
    def _():
        for ref in (halo_t, halo_m, halo_p, halo_1):
            ref[1] = jnp.zeros(ref.shape[1:], ref.dtype)

    def halo(low_src, high_src, dst, which):
        down = pltpu.make_async_remote_copy(
            src_ref=low_src, dst_ref=dst.at[1],
            send_sem=s_h.at[which, 0], recv_sem=r_h.at[which, 1],
            device_id={"tile": lax.max(tile - group, sub)}, device_id_type=MESH,
        )
        up = pltpu.make_async_remote_copy(
            src_ref=high_src, dst_ref=dst.at[0],
            send_sem=s_h.at[which, 1], recv_sem=r_h.at[which, 0],
            device_id={"tile": lax.min(tile + group, ntile - group + sub)}, device_id_type=MESH,
        )
        return down, up

    def halo_recv(copies):
        pl.when(has_low)(lambda: copies[1].wait_recv())
        pl.when(has_high)(lambda: copies[0].wait_recv())

    def halo_sent(copies):
        pl.when(has_low)(lambda: copies[0].wait_send())
        pl.when(has_high)(lambda: copies[1].wait_send())

    h_t = halo(col_t.at[0], col_t.at[grows - 1], halo_t, 0)
    h_m = halo(col_m.at[0], col_m.at[grows - 1], halo_m, 1)
    h_p = halo(pk.at[0], pk.at[group - 1], halo_p, 2)
    h_1 = halo(t1.at[0], t1.at[grows - 1], halo_1, 3)

    all_but_one(p1g, r_p1g)
    p1z[0] = jnp.zeros(p1z.shape[1:], jnp.float32)
    for t in range(ntier):
        acc = p1g[t * group, 0:1, :]
        for s in range(1, group):
            acc = acc + p1g[t * group + s, 0:1, :]
        p1z[0, t : t + 1, :] = acc
    acc = p1g[0, 1:2, :]
    for s in range(1, group):
        acc = acc + p1g[s, 1:2, :]
    p1z[0, ntier : ntier + 1, :] = acc
    across_send(p1z, s_p1z, r_p1z)

    for s, row in ((0, 0), (group - 1, grows - 1)):
        wait_for(col_t.at[row], r_et.at[s])
        wait_for(col_m.at[row], r_em.at[s])
    pl.when(has_low)(lambda: (h_m[0].start(), h_t[0].start()) and None)
    pl.when(has_high)(lambda: (h_m[1].start(), h_t[1].start()) and None)
    wait_for(pk, r_pk)
    pl.when(has_low)(lambda: h_p[0].start())
    pl.when(has_high)(lambda: h_p[1].start())

    inverse = 1.0 / ((2.0 * RATE) * rates[...])
    table = [
        [jnp.broadcast_to(inverse[a : a + 1, m : m + 1], (1, C)) for m in range(nmat)]
        for a in range(2)
    ]

    def lookup(codes, axes):
        outs = [jnp.broadcast_to(table[a][0], codes.shape) for a in axes]
        for m in range(1, nmat):
            hit = codes == m
            outs = [jnp.where(hit, table[a][m], o) for a, o in zip(axes, outs)]
        return outs

    def unpack(low, high, shift_low, shift_high, split):
        pieces = []
        for t in range(ntier):
            for g in range(lev // 8):
                a = roll(low(t), shift_low - 32 * g)
                if high is not None:
                    a = jnp.where(lane < split, a, roll(high(t), shift_high - 32 * g))
                pieces.append(a)
        return jnp.concatenate(pieces, axis=0)

    def swap(x):
        return jnp.where((lane & 3) == 1, roll(x, -1), roll(x, 1))

    half = 4 * rows
    out_t = unpack(lambda t: pk[0, t], lambda t: pk[1, t], 0, half, half)
    out_m = unpack(lambda t: pk[0, t], lambda t: pk[1, t], -half, 0, half)
    ixc, iyc = lookup(out_m, (0, 1))
    pos_low = (lane & 3) == 1

    wait_for(col_m.at[pl.ds(1, grows - 2)], r_rm)
    before = None
    inner = jnp.ones((levels, C), jnp.float32)
    for r in range(grows):
        ix, iy = lookup(col_m[r], (0, 1))
        cy[r] = 1.0 / (iy + roll(iy, -1))
        inner = jnp.where((lane >> 2) == r, roll(iy, 4 * r + 2), inner)
        if r == 0:
            first = ix
        else:
            cx[r] = 1.0 / (before + ix)
        before = ix
    last = before

    there_is = jnp.where(pos_low, jnp.where(own > 0, 1.0, 0.0), jnp.where(own < nwin - 1, 1.0, 0.0))
    c_in = there_is / (iyc + swap(inner))
    c_far = 1.0 / (iyc + jnp.where(pos_low, roll(iyc, 1), roll(iyc, -1)))
    spun = swap(c_in)
    for r in range(grows):
        ce[r] = roll(spun, -(4 * r + 2))
        cy[r] = jnp.where(lane == C - 1, ce[r], cy[r])

    halo_recv(h_m)
    halo_recv(h_p)
    (ix,) = lookup(halo_m[0], (0,))
    cx[0] = jnp.where(has_low, 1.0 / (ix + first), 0.0)
    (ix,) = lookup(halo_m[1], (0,))
    cx[grows] = jnp.where(has_high, 1.0 / (ix + last), 0.0)

    end = 4 * (rows - 1)
    up_t = unpack(lambda t: halo_p[0, t], None, -end, 0, 0)
    up_m = unpack(lambda t: halo_p[0, t], None, -end - half, 0, 0)
    dn_t = unpack(lambda t: halo_p[1, t], None, 4 * (grows - 1), 0, 0)
    dn_m = unpack(lambda t: halo_p[1, t], None, 4 * (grows - 1) - half, 0, 0)
    (up_ix,) = lookup(up_m, (0,))
    (dn_ix,) = lookup(dn_m, (0,))
    at_top = lane < 4
    at_bottom = lane >= 4 * (grows - 1)
    up_c = 1.0 / (ixc + jnp.where(at_top, up_ix, roll(ixc, 4)))
    up_c = jnp.where(jnp.logical_and(at_top, jnp.logical_not(has_low)), 0.0, up_c)
    dn_c = 1.0 / (ixc + jnp.where(at_bottom, dn_ix, roll(ixc, -4)))
    dn_c = jnp.where(jnp.logical_and(at_bottom, jnp.logical_not(has_high)), 0.0, dn_c)
    part = (
        out_t
        + up_c * (jnp.where(at_top, up_t, roll(out_t, 4)) - out_t)
        + dn_c * (jnp.where(at_bottom, dn_t, roll(out_t, -4)) - out_t)
        + c_far * (jnp.where(pos_low, roll(out_t, 1), roll(out_t, -1)) - out_t)
    )

    op = a_in[...]
    op_active = [op[:, a : a + 1] for a in active_rows]

    all_but_one(p1z, r_p1z)
    whole = total(p1z)
    count = whole[ntier : ntier + 1, 0:nblk]
    power = stat[...] * jnp.exp(fac[...] * whole[0:ntier, 0:nblk] / count)

    def label_of(s, w):
        return jnp.sum(jnp.where(lane == w, p1g[s, 2:3, 0:C], 0.0), axis=1, keepdims=True)

    blkf = blk.astype(jnp.float32)

    def gain_of(pw, label):
        return SOURCE_GAIN * jnp.sum(jnp.where(blkf == label, pw, 0.0), axis=1, keepdims=True)

    own_labels = [label_of(s, own) for s in range(group)]
    gains = [gain_of(power, label) for label in own_labels]
    lift = []
    for s in range(group):
        acc = op_active[0] * gains[s][0:1, :]
        for t in range(1, ntier):
            acc = acc + op_active[t] * gains[s][t : t + 1, :]
        lift.append(acc)
    side = jnp.zeros((ntier, C), jnp.float32)
    for s in range(group):
        gl = gain_of(power, label_of(s, own - 1))
        gr = gain_of(power, label_of(s, own + 1))
        side = jnp.where(lane // half == s, jnp.where(pos_low, gl, gr), side)
    lift_c = op_active[0] * side[0:1, :]
    for t in range(1, ntier):
        lift_c = lift_c + op_active[t] * side[t : t + 1, :]

    def lateral(field, outside, r, above, below):
        here = field[r]
        edge_in = roll(outside, -(4 * r + 2))
        beside = jnp.where(lane == C - 1, edge_in, roll(here, -1))
        flux = cy[r] * (beside - here)
        left = jnp.where(lane == 0, ce[r] * (here - edge_in), roll(flux, 1))
        moved = here + (flux - left)
        return moved + cx[r + 1] * (below - here) - cx[r] * (here - above)

    halo_recv(h_t)
    wait_for(col_t.at[pl.ds(1, grows - 2)], r_rt)
    spun = swap(out_t)
    inner = out_t
    for r in range(grows):
        above = halo_t[0] if r == 0 else col_t[r - 1]
        below = halo_t[1] if r == grows - 1 else col_t[r + 1]
        mv[:, r * C : (r + 1) * C] = lateral(col_t, spun, r, above, below)
        inner = jnp.where((lane >> 2) == r, roll(col_t[r], 4 * r + 2), inner)
    mv[:, grows * C : (grows + 1) * C] = part + c_in * (swap(inner) - out_t)

    order = [0, grows - 1] + list(range(1, grows - 1))
    for r in order:
        t1[r] = solve(op, mv[:, r * C : (r + 1) * C]) + lift[r // rows]
        if r == grows - 1:
            pl.when(has_low)(lambda: h_1[0].start())
            pl.when(has_high)(lambda: h_1[1].start())
    t1c = solve(op, mv[:, grows * C : (grows + 1) * C]) + lift_c

    p2g[own] = jnp.zeros(p2g.shape[1:], jnp.float32)
    sums = jnp.zeros((ntier, nblk), jnp.float32)
    for s in range(group):
        acc = []
        for a in active_rows:
            v = t1[s * rows, a : a + 1, :]
            for r in range(1, rows):
                v = v + t1[s * rows + r, a : a + 1, :]
            acc.append(v)
        acc = jnp.sum(jnp.concatenate(acc, axis=0), axis=1, keepdims=True)
        sums = sums + jnp.where(blkf == own_labels[s], acc, 0.0)
    p2g[own, 0:ntier, 0:nblk] = sums
    group_send(p2g, s_p2g, r_p2g)

    def send_rows(s, first_row, count):
        for t in range(ntier):
            for_me = jnp.logical_and(tier == t, sub == s)
            src_ref = res.at[pl.ds(s * rows + first_row, count), pl.ds(t * lev, lev), :]
            dst_ref = out.at[pl.ds(first_row, count), :, cols(own)]

            @pl.when(for_me)
            def _():
                pltpu.make_async_copy(src_ref, dst_ref, r_o).start()

            @pl.when(jnp.logical_not(for_me))
            def _():
                pltpu.make_async_remote_copy(
                    src_ref=src_ref, dst_ref=dst_ref, send_sem=s_o, recv_sem=r_o,
                    device_id=there(t, s), device_id_type=MESH,
                ).start()

    spun = swap(t1c)

    def finish(r):
        above = halo_1[0] if r == 0 else t1[r - 1]
        below = halo_1[1] if r == grows - 1 else t1[r + 1]
        mv[:, r * C : (r + 1) * C] = lateral(t1, spun, r, above, below)
        res[r] = solve(op, mv[:, r * C : (r + 1) * C])

    for s in range(group):
        for r in range(s * rows + (s == 0), (s + 1) * rows - (s == group - 1)):
            finish(r)
        send_rows(s, int(s == 0), rows - 1)

    all_but_one(p2g, r_p2g)
    acc = p2g[0]
    for k in range(1, nwin):
        acc = acc + p2g[k]
    p2z[0] = acc
    across_send(p2z, s_p2z, r_p2z)

    halo_recv(h_1)
    for s, r in ((0, 0), (group - 1, grows - 1)):
        finish(r)
        send_rows(s, r - s * rows, 1)

    all_but_one(p2z, r_p2z)
    whole = total(p2z)
    power = stat[...] * jnp.exp(fac[...] * whole[0:ntier, 0:nblk] / count)
    mine = lax.broadcasted_iota(jnp.int32, (ntier, nblk), 0) == tier
    pw_out[...] = jnp.sum(jnp.where(mine, power, 0.0), axis=0, keepdims=True)
    own_op = a_in[levs(tier), :]
    lifts = []
    for j in range(width // C):
        g = SOURCE_GAIN * jnp.sum(jnp.where(blk == labels[0, j], power, 0.0), axis=1, keepdims=True)
        acc = own_op[:, active_rows[0] : active_rows[0] + 1] * g[0:1, :]
        for t in range(1, ntier):
            a = active_rows[t]
            acc = acc + own_op[:, a : a + 1] * g[t : t + 1, :]
        lifts.append(acc)

    wait_for(out, r_o)
    for j in range(width // C):
        for r in range(rows):
            out[r, :, j * C : (j + 1) * C] += lifts[j]

    for copies in (h_t, h_m, h_p, h_1):
        halo_sent(copies)
    sent = pl.ds(0, nwin - 1)
    wait_for(res.at[sent], s_t)
    wait_for(res.at[sent], s_m)
    wait_for(res.at[sent], s_o)
    wait_for(pk_out.at[sent, 0], s_pk)
    all_but_one(p1g, s_p1g)
    all_but_one(p2g, s_p2g)
    all_but_one(p1z, s_p1z)
    all_but_one(p2z, s_p2z)


def solution(mesh):
    ntier, ntile = mesh.shape["tier"], mesh.shape["tile"]

    def shards(temp, mats, rates, labels, stat, fac, op):
        rows, lev, width = temp.shape
        nblk = stat.shape[1]
        pad = -(-nblk // 128) * 128
        group = width // (ntier * C)
        levels, grows, ngrp, nwin = lev * ntier, rows * group, ntile // group, width // C
        f32, i32 = jnp.float32, jnp.int32
        vm = lambda shape, dtype=f32: pltpu.VMEM(shape, dtype)
        dma = pltpu.SemaphoreType.DMA
        vmem = pl.BlockSpec(memory_space=pltpu.VMEM)
        field = (grows, levels, C)
        return pl.pallas_call(
            functools.partial(kernel, ntier, ntile, nblk, group),
            out_shape=(
                jax.ShapeDtypeStruct(temp.shape, f32),
                jax.ShapeDtypeStruct((1, nblk), f32),
            ),
            in_specs=[pl.BlockSpec(memory_space=pltpu.HBM)] * 7,
            out_specs=(vmem, vmem),
            scratch_shapes=[
                vm(temp.shape), vm(mats.shape, i32), vm(rates.shape),
                pltpu.SMEM(labels.shape, i32), vm(stat.shape), vm(fac.shape), vm(op.shape),
                dma((7,)),
                vm(field), vm(field, i32), vm((2, levels, C)), vm((2, levels, C), i32), vm((2, levels, C)),
                vm((nwin, lev // 8, 8, C)), vm((group, ntier, 8, C)), vm((2, ntier, 8, C)),
                vm((grows + 1, levels, C)), vm(field), vm(field), vm((levels, (grows + 1) * C)),
                vm(field), vm((levels, C)), vm(field),
                vm((nwin, 8, pad)), vm((ngrp, 8, pad)), vm((nwin, 8, pad)), vm((ngrp, 8, pad)),
                dma, dma, dma, dma,
                dma((group,)), dma((group,)), dma, dma, dma, dma,
                dma((4, 2)), dma((4, 2)),
                dma, dma, dma, dma, dma, dma, dma, dma,
            ],
            compiler_params=pltpu.CompilerParams(
                collective_id=0, has_side_effects=True, vmem_limit_bytes=62 * 1024 * 1024
            ),
        )(temp, mats, rates, labels, stat, fac, op)

    return jax.shard_map(
        shards,
        mesh=mesh,
        in_specs=(P("tile", "tier", None), P("tile", "tier", None), P(), P("tile", None), P(), P(), P()),
        out_specs=(P("tile", "tier", None), P("tier", None)),
        check_vma=False,
    )
```

time: 35.2 us -> 28.8 us (0.82)
  Pallas kernels: 32.1 us -> 25.8 us
    pallas_call x1, Pallas kernels: 32.1 us -> 25.8 us  [shards(): pl.pallas_call(functools.partial(kernel, ntier, ntile, nblk, group), out_...]
where the time goes in v1:
time: 28.8 us; the launch traced here: 28.7 us
  Pallas kernels  25.8 us (90%)
  local copies, waits for them, and re-layouts  2.28 us (8%)
  between operations  0.65 us (2%)
    pallas_call x1, Pallas kernels, shards(): pl.pallas_call(functools.partial(kernel, ntier, ntile, nblk, group), out_...  25.8 us
    unnamed x4, local copies, waits for them, and re-layouts  2.28 us

profile of v1, /device:TPU:0, one launch (start us, length us, event | category | flops | bytes accessed | tf_op | source)
XLA Modules:
  0.0 28.7 jit_solution(17162214743341265981)
XLA Ops:
  0.6 25.8 %shard_map.86 = (f32[4,24,1024]{2,1,0:T(8,128)}, f32[1,16]{1,0:T(1,128)}) custom-call(f32[4,24,1024]{2,1,0:T(8,128)} %t_hbm.1, s32[4,24,1024]{2,1,0:T(8,128)} %m_hbm.1, f32[2,8]{1,0:T(2,128)} %rates_hbm.1, s32[1,8]{1,0:T(1,128)} %labels_hbm.1, f32[4,16]{1,0:T(4,128)} %stat_hbm.1, f32[4,16]{1,0:T(4,128)} %fac_hbm.1, f32[96,96]{1,0:T(8,128)} %a_hbm.1), custom_call_target="tpu_custom_call" | custom-call | tf_op jit(solution)/shard_map/pallas_call | solution.py:510
  26.4 0.0 copy-start
  26.4 1.8 %copy.11 = f32[4,24,1024]{2,1,0:T(8,128)} copy(f32[4,24,1024]{2,1,0:T(8,128)} %get-tuple-element.4) | data formatting | bytes 786432
  28.2 0.0 copy-done
  28.2 0.5 %copy.12 = f32[1,16]{1,0:T(1,128)} copy(f32[1,16]{1,0:T(1,128)S(1)} %copy-done) | data formatting | bytes 128
Async XLA Ops:
  26.4 1.8 %copy-start = (f32[1,16]{1,0:T(1,128)S(1)}, f32[1,16]{1,0:T(1,128)}, u32[]{:S(2)}) copy-start(f32[1,16]{1,0:T(1,128)} %get-tuple-element.5) | copy-start | bytes 196

commit v2 on v1

--- a/solution.py
+++ b/solution.py
@@ -24,7 +24,7 @@
 def kernel(
     ntier, ntile, nblk, group,
     t_hbm, m_hbm, rates_hbm, labels_hbm, stat_hbm, fac_hbm, a_hbm,
-    out, pw_out,
+    out, pw_out, lift_out,
     t_in, m_in, rates, labels, stat, fac, a_in, s_in,
     col_t, col_m, halo_t, halo_m, halo_1,
     pk_out, pk, halo_p,
@@ -466,19 +466,14 @@
     mine = lax.broadcasted_iota(jnp.int32, (ntier, nblk), 0) == tier
     pw_out[...] = jnp.sum(jnp.where(mine, power, 0.0), axis=0, keepdims=True)
     own_op = a_in[levs(tier), :]
-    lifts = []
     for j in range(width // C):
         g = SOURCE_GAIN * jnp.sum(jnp.where(blk == labels[0, j], power, 0.0), axis=1, keepdims=True)
         acc = own_op[:, active_rows[0] : active_rows[0] + 1] * g[0:1, :]
         for t in range(1, ntier):
             a = active_rows[t]
             acc = acc + own_op[:, a : a + 1] * g[t : t + 1, :]
-        lifts.append(acc)
-
+        lift_out[:, j * C : (j + 1) * C] = jnp.broadcast_to(acc, (lev, C))
     wait_for(out, r_o)
-    for j in range(width // C):
-        for r in range(rows):
-            out[r, :, j * C : (j + 1) * C] += lifts[j]
 
     for copies in (h_t, h_m, h_p, h_1):
         halo_sent(copies)
@@ -493,6 +488,18 @@
     all_but_one(p2z, s_p2z)
 
 
+def last(field, lift, power, out, power_out, done, sem):
+    copies = []
+    for r in range(field.shape[0]):
+        done[r] = field[r] + lift[...]
+        copies.append(pltpu.make_async_copy(done.at[r], out.at[r], sem.at[r]))
+        copies[-1].start()
+    copies.append(pltpu.make_async_copy(power, power_out, sem.at[field.shape[0]]))
+    copies[-1].start()
+    for copy in copies:
+        copy.wait()
+
+
 def solution(mesh):
     ntier, ntile = mesh.shape["tier"], mesh.shape["tile"]
 
@@ -506,23 +513,22 @@
         vm = lambda shape, dtype=f32: pltpu.VMEM(shape, dtype)
         dma = pltpu.SemaphoreType.DMA
         vmem = pl.BlockSpec(memory_space=pltpu.VMEM)
-        field = (grows, levels, C)
-        return pl.pallas_call(
+        block = (grows, levels, C)
+        args = (temp, mats, rates, labels, stat, fac, op)
+        args = [pltpu.with_memory_space_constraint(x, pltpu.HBM) for x in args]
+        field, power, lift = pl.pallas_call(
             functools.partial(kernel, ntier, ntile, nblk, group),
-            out_shape=(
-                jax.ShapeDtypeStruct(temp.shape, f32),
-                jax.ShapeDtypeStruct((1, nblk), f32),
-            ),
+            out_shape=(vm(temp.shape), vm((1, nblk)), vm((lev, width))),
             in_specs=[pl.BlockSpec(memory_space=pltpu.HBM)] * 7,
-            out_specs=(vmem, vmem),
+            out_specs=(vmem, vmem, vmem),
             scratch_shapes=[
                 vm(temp.shape), vm(mats.shape, i32), vm(rates.shape),
                 pltpu.SMEM(labels.shape, i32), vm(stat.shape), vm(fac.shape), vm(op.shape),
                 dma((7,)),
-                vm(field), vm(field, i32), vm((2, levels, C)), vm((2, levels, C), i32), vm((2, levels, C)),
+                vm(block), vm(block, i32), vm((2, levels, C)), vm((2, levels, C), i32), vm((2, levels, C)),
                 vm((nwin, lev // 8, 8, C)), vm((group, ntier, 8, C)), vm((2, ntier, 8, C)),
-                vm((grows + 1, levels, C)), vm(field), vm(field), vm((levels, (grows + 1) * C)),
-                vm(field), vm((levels, C)), vm(field),
+                vm((grows + 1, levels, C)), vm(block), vm(block), vm((levels, (grows + 1) * C)),
+                vm(block), vm((levels, C)), vm(block),
                 vm((nwin, 8, pad)), vm((ngrp, 8, pad)), vm((nwin, 8, pad)), vm((ngrp, 8, pad)),
                 dma, dma, dma, dma,
                 dma((group,)), dma((group,)), dma, dma, dma, dma,
@@ -530,9 +536,21 @@
                 dma, dma, dma, dma, dma, dma, dma, dma,
             ],
             compiler_params=pltpu.CompilerParams(
-                collective_id=0, has_side_effects=True, vmem_limit_bytes=62 * 1024 * 1024
+                collective_id=0, has_side_effects=True, vmem_limit_bytes=48 * 1024 * 1024
             ),
-        )(temp, mats, rates, labels, stat, fac, op)
+        )(*args)
+        anywhere = pl.BlockSpec(memory_space=pltpu.HBM)
+        return pl.pallas_call(
+            last,
+            out_shape=(
+                jax.ShapeDtypeStruct(temp.shape, f32),
+                jax.ShapeDtypeStruct((1, nblk), f32),
+            ),
+            in_specs=[vmem] * 3,
+            out_specs=(anywhere, anywhere),
+            scratch_shapes=[vm(temp.shape), dma((rows + 1,))],
+            compiler_params=pltpu.CompilerParams(vmem_limit_bytes=4 * 1024 * 1024),
+        )(field, lift, power)
 
     return jax.shard_map(
         shards,

time: 28.8 us -> 26.6 us (0.924)
  local copies, waits for them, and re-layouts: 2.28 us -> 0 us
    unnamed x4 -> x0, local copies, waits for them, and re-layouts: 2.28 us -> none
    pallas_call x0 -> x1, Pallas kernels: none -> 0.8 us  [shards(): pl.pallas_call(last, out_shape=(jax.ShapeDtypeStruct(temp.shape, f32), ja...]
    pallas_call x1, Pallas kernels: 25.8 us -> 25.1 us  [shards(): pl.pallas_call(functools.partial(kernel, ntier, ntile, nblk, group), out_...]
where the time goes in v2:
time: 26.6 us; the launch traced here: 26.5 us
  Pallas kernels  25.9 us (97%)
  between operations  0.64 us (2%)
    pallas_call x1, Pallas kernels, shards(): pl.pallas_call(functools.partial(kernel, ntier, ntile, nblk, group), out_...  25.1 us
    pallas_call x1, Pallas kernels, shards(): pl.pallas_call(last, out_shape=(jax.ShapeDtypeStruct(temp.shape, f32), ja...  0.8 us

profile of v2, /device:TPU:0, one launch (start us, length us, event | category | flops | bytes accessed | tf_op | source)
XLA Modules:
  0.0 26.5 jit_solution(4603399053110163871)
XLA Ops:
  0.6 25.1 %shard_map.86 = (f32[4,24,1024]{2,1,0:T(8,128)S(1)}, f32[1,16]{1,0:T(1,128)S(1)}, f32[24,1024]{1,0:T(8,128)S(1)}) custom-call(f32[4,24,1024]{2,1,0:T(8,128)} %t_hbm.1, s32[4,24,1024]{2,1,0:T(8,128)} %m_hbm.1, f32[2,8]{1,0:T(2,128)} %rates_hbm.1, s32[1,8]{1,0:T(1,128)} %labels_hbm.1, f32[4,16]{1,0:T(4,128)} %stat_hbm.1, f32[4,16]{1,0:T(4,128)} %fac_hbm.1, ...), custom_call_target="tpu_custom_call" | custom-call | tf_op jit(solution)/shard_map/pallas_call | solution.py:519
  25.7 0.8 %shard_map.87 = (f32[4,24,1024]{2,1,0:T(8,128)}, f32[1,16]{1,0:T(1,128)}) custom-call(f32[4,24,1024]{2,1,0:T(8,128)S(1)} %get-tuple-element.5.field, f32[24,1024]{1,0:T(8,128)S(1)} %get-tuple-element.6.lift, f32[1,16]{1,0:T(1,128)S(1)} %get-tuple-element.7.power), custom_call_target="tpu_custom_call" | custom-call | tf_op jit(solution)/shard_map/pallas_call | solution.py:543

commit v3 on v2

--- a/solution.py
+++ b/solution.py
@@ -13,8 +13,17 @@
 MESH = pl.DeviceIdType.MESH
 
 
+def split(x):
+    high = x.astype(jnp.bfloat16)
+    return high, (x - high.astype(jnp.float32)).astype(jnp.bfloat16)
+
+
 def solve(op, x):
-    return jnp.dot(op, x, precision=lax.Precision.HIGHEST, preferred_element_type=jnp.float32)
+    high, low = split(x)
+    n = op.shape[0] // 2
+    both = jnp.dot(op, high, preferred_element_type=jnp.float32)
+    more = jnp.dot(op[:n], low, preferred_element_type=jnp.float32)
+    return both[:n] + (both[n:] + more)
 
 
 def roll(x, shift):
@@ -31,9 +40,9 @@
     cx, cy, ce, mv, t1, t1c, res,
     p1g, p1z, p2g, p2z,
     s_t, s_m, s_pk, s_o,
-    r_et, r_em, r_rt, r_rm, r_pk, r_o,
+    r_et, r_em, r_at, r_am, r_it, r_rt, r_rm, r_pk, r_o,
     s_h, r_h,
-    s_p1g, r_p1g, s_p1z, r_p1z, s_p2g, r_p2g, s_p2z, r_p2z,
+    s_p1g, r_p1g, s_p1z, r_p1z, s_p2g, r_p2g, s_p2z, r_p2z, entered,
 ):
     tier = lax.axis_index("tier")
     tile = lax.axis_index("tile")
@@ -77,11 +86,16 @@
     def across(k):
         return {"tile": lax.rem(tile + k * group, ntile)}
 
-    def greet(k, carry):
-        pl.semaphore_signal(barrier, inc=1, device_id=across(k), device_id_type=MESH)
-        return carry
-
-    lax.fori_loop(1, ngrp, greet, 0)
+    def greet(sem, low, high):
+        def one(k, carry):
+            pl.semaphore_signal(
+                sem, inc=1, device_id={"tile": k * group + sub}, device_id_type=MESH
+            )
+            return carry
+
+        lax.fori_loop(low, high, one, 0)
+
+    greet(barrier, place + 1, ngrp)
 
     def cols(w):
         return pl.ds(pl.multiple_of(w * C, C), C)
@@ -112,7 +126,8 @@
     p1g[own, 1:2, 0:nblk] = areas
     p1g[own, 2:3, 0:C] = names
 
-    pl.semaphore_wait(barrier, nwin - 1 + ngrp - 1)
+    pl.semaphore_wait(barrier, nwin - 1 + place)
+    greet(entered, 0, place)
 
     def group_send(buf, s_sem, r_sem):
         for mine, t2, s2 in peers:
@@ -156,7 +171,10 @@
                 ).start()
 
     edge = lax.select(sub == 0, 0, rows - 1)
-    rest = lax.select(sub == 0, 1, 0)
+    beside = lax.select(sub == 0, 1, rows - 2)
+    rest = lax.select(sub == 0, 2, 0)
+    inmost = lax.select(sub == 0, rows - 1, 0)
+    other = lax.select(sub == 0, rows - 2, 1)
     spread(t_hbm, col_t, edge, sub * rows + edge, 1, s_t, r_et.at[sub])
     spread(m_hbm, col_m, edge, sub * rows + edge, 1, s_m, r_em.at[sub])
 
@@ -164,9 +182,9 @@
     for w in range(nwin):
         low = max(w - 1, 0) * C
         high = min(w + 1, nwin - 1) * C
+        first = second = None
         for g in range(lev // 8):
             ls = slice(8 * g, 8 * g + 8)
-            acc = None
             for q, src in ((0, t_in), (rows, m_in)):
                 for r in range(rows):
                     both = jnp.where(
@@ -175,22 +193,20 @@
                     if q:
                         both = both.astype(jnp.float32)
                     put = roll(both, 32 * g + 4 * (q + r) + 2)
-                    acc = put if acc is None else jnp.where(quad == 8 * g + q + r, put, acc)
-            pk_out[w, g] = acc
-
-    def fold(w):
-        total_p = None
-        for g in range(lev // 8):
-            piece = pk_out[w, g]
-            keep = (lane >= 32 * g) & (lane < 32 * g + 32)
-            total_p = jnp.where(keep, piece, 0.0) if total_p is None else jnp.where(keep, piece, total_p)
-        return total_p
-
-    for w in range(nwin):
-        pk_out[w, 0] = fold(w)
+                    first = put if first is None else jnp.where(quad == 8 * g + q + r, put, first)
+            whole = None
+            for r in range(rows):
+                block = t_in[r, ls, w * C : (w + 1) * C]
+                whole = block if whole is None else whole + block
+                put = roll(block, 32 * g + 4 * r + 2)
+                second = put if second is None else jnp.where(quad == 8 * g + r, put, second)
+            whole = jnp.sum(whole, axis=1, keepdims=True)
+            second = jnp.where(lane == 32 * g + 3, whole, second)
+        pk_out[w, 0] = first
+        pk_out[w, 1] = second
 
     for mine, t2, s2 in peers:
-        src_ref, dst_ref = pk_out.at[t2 * group + s2, 0], pk.at[sub, tier]
+        src_ref, dst_ref = pk_out.at[t2 * group + s2], pk.at[sub, tier]
         if mine:
             pltpu.make_async_copy(src_ref, dst_ref, r_pk).start()
         else:
@@ -198,8 +214,11 @@
                 src_ref=src_ref, dst_ref=dst_ref, send_sem=s_pk, recv_sem=r_pk,
                 device_id=there(t2, s2), device_id_type=MESH,
             ).start()
-    spread(m_hbm, col_m, rest, sub * rows + rest, rows - 1, s_m, r_rm)
-    spread(t_hbm, col_t, rest, sub * rows + rest, rows - 1, s_t, r_rt)
+    spread(m_hbm, col_m, beside, sub * rows + beside, 1, s_m, r_am.at[sub])
+    spread(t_hbm, col_t, beside, sub * rows + beside, 1, s_t, r_at.at[sub])
+    spread(m_hbm, col_m, rest, sub * rows + rest, rows - 2, s_m, r_rm)
+    spread(t_hbm, col_t, inmost, sub * rows + inmost, 1, s_t, r_it)
+    spread(t_hbm, col_t, other, sub * rows + other, 1, s_t, r_rt.at[sub])
 
     has_low = place > 0
     has_high = place < ngrp - 1
@@ -251,6 +270,7 @@
     for s in range(1, group):
         acc = acc + p1g[s, 1:2, :]
     p1z[0, ntier : ntier + 1, :] = acc
+    pl.when(has_high)(lambda: pl.semaphore_wait(entered, ngrp - 1 - place))
     across_send(p1z, s_p1z, r_p1z)
 
     for s, row in ((0, 0), (group - 1, grows - 1)):
@@ -289,62 +309,14 @@
         return jnp.where((lane & 3) == 1, roll(x, -1), roll(x, 1))
 
     half = 4 * rows
-    out_t = unpack(lambda t: pk[0, t], lambda t: pk[1, t], 0, half, half)
-    out_m = unpack(lambda t: pk[0, t], lambda t: pk[1, t], -half, 0, half)
+    out_t = unpack(lambda t: pk[0, t, 0], lambda t: pk[1, t, 0], 0, half, half)
+    out_m = unpack(lambda t: pk[0, t, 0], lambda t: pk[1, t, 0], -half, 0, half)
+    own_t = unpack(lambda t: pk[0, t, 1], lambda t: pk[1, t, 1], 0, half, half)
     ixc, iyc = lookup(out_m, (0, 1))
     pos_low = (lane & 3) == 1
 
-    wait_for(col_m.at[pl.ds(1, grows - 2)], r_rm)
-    before = None
-    inner = jnp.ones((levels, C), jnp.float32)
-    for r in range(grows):
-        ix, iy = lookup(col_m[r], (0, 1))
-        cy[r] = 1.0 / (iy + roll(iy, -1))
-        inner = jnp.where((lane >> 2) == r, roll(iy, 4 * r + 2), inner)
-        if r == 0:
-            first = ix
-        else:
-            cx[r] = 1.0 / (before + ix)
-        before = ix
-    last = before
-
-    there_is = jnp.where(pos_low, jnp.where(own > 0, 1.0, 0.0), jnp.where(own < nwin - 1, 1.0, 0.0))
-    c_in = there_is / (iyc + swap(inner))
-    c_far = 1.0 / (iyc + jnp.where(pos_low, roll(iyc, 1), roll(iyc, -1)))
-    spun = swap(c_in)
-    for r in range(grows):
-        ce[r] = roll(spun, -(4 * r + 2))
-        cy[r] = jnp.where(lane == C - 1, ce[r], cy[r])
-
-    halo_recv(h_m)
-    halo_recv(h_p)
-    (ix,) = lookup(halo_m[0], (0,))
-    cx[0] = jnp.where(has_low, 1.0 / (ix + first), 0.0)
-    (ix,) = lookup(halo_m[1], (0,))
-    cx[grows] = jnp.where(has_high, 1.0 / (ix + last), 0.0)
-
-    end = 4 * (rows - 1)
-    up_t = unpack(lambda t: halo_p[0, t], None, -end, 0, 0)
-    up_m = unpack(lambda t: halo_p[0, t], None, -end - half, 0, 0)
-    dn_t = unpack(lambda t: halo_p[1, t], None, 4 * (grows - 1), 0, 0)
-    dn_m = unpack(lambda t: halo_p[1, t], None, 4 * (grows - 1) - half, 0, 0)
-    (up_ix,) = lookup(up_m, (0,))
-    (dn_ix,) = lookup(dn_m, (0,))
-    at_top = lane < 4
-    at_bottom = lane >= 4 * (grows - 1)
-    up_c = 1.0 / (ixc + jnp.where(at_top, up_ix, roll(ixc, 4)))
-    up_c = jnp.where(jnp.logical_and(at_top, jnp.logical_not(has_low)), 0.0, up_c)
-    dn_c = 1.0 / (ixc + jnp.where(at_bottom, dn_ix, roll(ixc, -4)))
-    dn_c = jnp.where(jnp.logical_and(at_bottom, jnp.logical_not(has_high)), 0.0, dn_c)
-    part = (
-        out_t
-        + up_c * (jnp.where(at_top, up_t, roll(out_t, 4)) - out_t)
-        + dn_c * (jnp.where(at_bottom, dn_t, roll(out_t, -4)) - out_t)
-        + c_far * (jnp.where(pos_low, roll(out_t, 1), roll(out_t, -1)) - out_t)
-    )
-
-    op = a_in[...]
-    op_active = [op[:, a : a + 1] for a in active_rows]
+    op_active = [a_in[:, a : a + 1] for a in active_rows]
+    op = jnp.concatenate(split(a_in[...]), axis=0)
 
     all_but_one(p1z, r_p1z)
     whole = total(p1z)
@@ -376,6 +348,76 @@
     for t in range(1, ntier):
         lift_c = lift_c + op_active[t] * side[t : t + 1, :]
 
+    kx = {}
+    inner = {}
+    far = jnp.ones((levels, C), jnp.float32)
+
+    def conduct(r):
+        kx[r], iy = lookup(col_m[r], (0, 1))
+        cy[r] = 1.0 / (iy + roll(iy, -1))
+        inner[r] = roll(iy, 4 * r + 2)
+        for q in (r, r + 1):
+            if q - 1 in kx and q in kx:
+                cx[q] = 1.0 / (kx[q - 1] + kx[q])
+
+    there_is = jnp.where(pos_low, jnp.where(own > 0, 1.0, 0.0), jnp.where(own < nwin - 1, 1.0, 0.0))
+
+    def sideways(rs):
+        at = jnp.ones((levels, C), jnp.float32)
+        for r in rs:
+            at = jnp.where((lane >> 2) == r, inner[r], at)
+        c_in = there_is / (iyc + swap(at))
+        spun = swap(c_in)
+        for r in rs:
+            ce[r] = roll(spun, -(4 * r + 2))
+            cy[r] = jnp.where(lane == C - 1, ce[r], cy[r])
+        return c_in
+
+    c_far = 1.0 / (iyc + jnp.where(pos_low, roll(iyc, 1), roll(iyc, -1)))
+
+    outer = [0, grows - 1]
+    near = [1, grows - 2]
+    middle = list(range(2, grows - 2))
+    for s, row in ((0, 1), (group - 1, grows - 2)):
+        wait_for(col_m.at[row], r_am.at[s])
+    for r in outer + near:
+        conduct(r)
+    wait_for(col_m.at[pl.ds(2, grows - 4)], r_rm)
+    for r in middle:
+        conduct(r)
+    first, last = kx[0], kx[grows - 1]
+    c_in = sideways(range(grows))
+    into_side = c_in * (swap(own_t) - out_t)
+
+    halo_recv(h_m)
+    halo_recv(h_p)
+    (ix,) = lookup(halo_m[0], (0,))
+    cx[0] = jnp.where(has_low, 1.0 / (ix + first), 0.0)
+    (ix,) = lookup(halo_m[1], (0,))
+    cx[grows] = jnp.where(has_high, 1.0 / (ix + last), 0.0)
+
+    end = 4 * (rows - 1)
+    up_t = unpack(lambda t: halo_p[0, t, 0], None, -end, 0, 0)
+    up_m = unpack(lambda t: halo_p[0, t, 0], None, -end - half, 0, 0)
+    dn_t = unpack(lambda t: halo_p[1, t, 0], None, 4 * (grows - 1), 0, 0)
+    dn_m = unpack(lambda t: halo_p[1, t, 0], None, 4 * (grows - 1) - half, 0, 0)
+    (up_ix,) = lookup(up_m, (0,))
+    (dn_ix,) = lookup(dn_m, (0,))
+    at_top = lane < 4
+    at_bottom = lane >= 4 * (grows - 1)
+    up_c = 1.0 / (ixc + jnp.where(at_top, up_ix, roll(ixc, 4)))
+    up_c = jnp.where(jnp.logical_and(at_top, jnp.logical_not(has_low)), 0.0, up_c)
+    dn_c = 1.0 / (ixc + jnp.where(at_bottom, dn_ix, roll(ixc, -4)))
+    dn_c = jnp.where(jnp.logical_and(at_bottom, jnp.logical_not(has_high)), 0.0, dn_c)
+    part = (
+        out_t
+        + up_c * (jnp.where(at_top, up_t, roll(out_t, 4)) - out_t)
+        + dn_c * (jnp.where(at_bottom, dn_t, roll(out_t, -4)) - out_t)
+        + into_side
+        + c_far * (jnp.where(pos_low, roll(out_t, 1), roll(out_t, -1)) - out_t)
+    )
+
+
     def lateral(field, outside, r, above, below):
         here = field[r]
         edge_in = roll(outside, -(4 * r + 2))
@@ -386,37 +428,69 @@
         return moved + cx[r + 1] * (below - here) - cx[r] * (here - above)
 
     halo_recv(h_t)
-    wait_for(col_t.at[pl.ds(1, grows - 2)], r_rt)
     spun = swap(out_t)
-    inner = out_t
-    for r in range(grows):
+    place_of = {r: i for i, r in enumerate(outer + [grows] + list(range(1, grows - 1)))}
+
+    def at(r, n=1):
+        return slice(place_of[r] * C, (place_of[r] + n) * C)
+
+    def first_move(r):
         above = halo_t[0] if r == 0 else col_t[r - 1]
         below = halo_t[1] if r == grows - 1 else col_t[r + 1]
-        mv[:, r * C : (r + 1) * C] = lateral(col_t, spun, r, above, below)
-        inner = jnp.where((lane >> 2) == r, roll(col_t[r], 4 * r + 2), inner)
-    mv[:, grows * C : (grows + 1) * C] = part + c_in * (swap(inner) - out_t)
-
-    order = [0, grows - 1] + list(range(1, grows - 1))
-    for r in order:
-        t1[r] = solve(op, mv[:, r * C : (r + 1) * C]) + lift[r // rows]
-        if r == grows - 1:
-            pl.when(has_low)(lambda: h_1[0].start())
-            pl.when(has_high)(lambda: h_1[1].start())
-    t1c = solve(op, mv[:, grows * C : (grows + 1) * C]) + lift_c
-
+        mv[:, at(r)] = lateral(col_t, spun, r, above, below)
+
+    for s, row in ((0, 1), (group - 1, grows - 2)):
+        wait_for(col_t.at[row], r_at.at[s])
+    for r in outer:
+        first_move(r)
+    mv[:, at(grows)] = part
+    both = solve(op, mv[:, at(0, 3)])
+    for i, r in enumerate(outer):
+        t1[r] = both[:, i * C : (i + 1) * C] + lift[r // rows]
+    t1c = both[:, 2 * C :] + lift_c
+    pl.when(has_low)(lambda: h_1[0].start())
+    pl.when(has_high)(lambda: h_1[1].start())
+
+    wait_for(col_t.at[pl.ds(rows - 1, 2)], r_it)
+    flows = [
+        cx[0] * (halo_t[0] - col_t[0]),
+        cx[rows] * (col_t[rows] - col_t[rows - 1]),
+        cx[grows] * (halo_t[1] - col_t[grows - 1]),
+    ]
+    inflow = (flows[0] + flows[1], flows[2] - flows[1])
+    side_lane = jnp.logical_or((lane & 3) == 1, (lane & 3) == 2)
+    stock = []
+    for s in range(group):
+        mine = jnp.logical_and(lane // half == s, side_lane)
+        stock.append(
+            inflow[s]
+            - jnp.where(mine, into_side, 0.0)
+            + jnp.where(lane == s * half + 3, own_t, 0.0)
+        )
+    n_act = -(-ntier // 8) * 8
+    act = jnp.concatenate(
+        [a_in[a : a + 1, :] for a in active_rows]
+        + [jnp.zeros((n_act - ntier, levels), jnp.float32)], axis=0
+    )
+    found = solve(jnp.concatenate(split(act), axis=0), jnp.concatenate(stock, axis=1))
     p2g[own] = jnp.zeros(p2g.shape[1:], jnp.float32)
     sums = jnp.zeros((ntier, nblk), jnp.float32)
     for s in range(group):
-        acc = []
-        for a in active_rows:
-            v = t1[s * rows, a : a + 1, :]
-            for r in range(1, rows):
-                v = v + t1[s * rows + r, a : a + 1, :]
-            acc.append(v)
-        acc = jnp.sum(jnp.concatenate(acc, axis=0), axis=1, keepdims=True)
+        acc = jnp.sum(found[0:ntier, s * C : (s + 1) * C], axis=1, keepdims=True)
+        acc = acc + float(rows * C) * jnp.concatenate(
+            [lift[s][a : a + 1, :] for a in active_rows], axis=0
+        )
         sums = sums + jnp.where(blkf == own_labels[s], acc, 0.0)
     p2g[own, 0:ntier, 0:nblk] = sums
     group_send(p2g, s_p2g, r_p2g)
+
+    for s, row in ((0, rows - 2), (group - 1, rows + 1)):
+        wait_for(col_t.at[row], r_rt.at[s])
+    for r in near + middle:
+        first_move(r)
+    most = solve(op, mv[:, at(1, grows - 2)])
+    for r in range(1, grows - 1):
+        t1[r] = most[:, (r - 1) * C : r * C] + lift[r // rows]
 
     def send_rows(s, first_row, count):
         for t in range(ntier):
@@ -437,15 +511,17 @@
 
     spun = swap(t1c)
 
-    def finish(r):
-        above = halo_1[0] if r == 0 else t1[r - 1]
-        below = halo_1[1] if r == grows - 1 else t1[r + 1]
-        mv[:, r * C : (r + 1) * C] = lateral(t1, spun, r, above, below)
-        res[r] = solve(op, mv[:, r * C : (r + 1) * C])
+    def finish(rs):
+        for r in rs:
+            above = halo_1[0] if r == 0 else t1[r - 1]
+            below = halo_1[1] if r == grows - 1 else t1[r + 1]
+            mv[:, at(r)] = lateral(t1, spun, r, above, below)
+        x = solve(op, mv[:, at(rs[0], len(rs))])
+        for i, r in enumerate(rs):
+            res[r] = x[:, i * C : (i + 1) * C]
 
     for s in range(group):
-        for r in range(s * rows + (s == 0), (s + 1) * rows - (s == group - 1)):
-            finish(r)
+        finish(list(range(s * rows + (s == 0), (s + 1) * rows - (s == group - 1))))
         send_rows(s, int(s == 0), rows - 1)
 
     all_but_one(p2g, r_p2g)
@@ -456,8 +532,8 @@
     across_send(p2z, s_p2z, r_p2z)
 
     halo_recv(h_1)
+    finish(outer)
     for s, r in ((0, 0), (group - 1, grows - 1)):
-        finish(r)
         send_rows(s, r - s * rows, 1)
 
     all_but_one(p2z, r_p2z)
@@ -481,10 +557,10 @@
     wait_for(res.at[sent], s_t)
     wait_for(res.at[sent], s_m)
     wait_for(res.at[sent], s_o)
-    wait_for(pk_out.at[sent, 0], s_pk)
+    wait_for(pk_out.at[sent], s_pk)
     all_but_one(p1g, s_p1g)
+    all_but_one(p1z, s_p1z)
     all_but_one(p2g, s_p2g)
-    all_but_one(p1z, s_p1z)
     all_but_one(p2z, s_p2z)
 
 
@@ -526,14 +602,14 @@
                 pltpu.SMEM(labels.shape, i32), vm(stat.shape), vm(fac.shape), vm(op.shape),
                 dma((7,)),
                 vm(block), vm(block, i32), vm((2, levels, C)), vm((2, levels, C), i32), vm((2, levels, C)),
-                vm((nwin, lev // 8, 8, C)), vm((group, ntier, 8, C)), vm((2, ntier, 8, C)),
+                vm((nwin, 2, 8, C)), vm((group, ntier, 2, 8, C)), vm((2, ntier, 2, 8, C)),
                 vm((grows + 1, levels, C)), vm(block), vm(block), vm((levels, (grows + 1) * C)),
                 vm(block), vm((levels, C)), vm(block),
                 vm((nwin, 8, pad)), vm((ngrp, 8, pad)), vm((nwin, 8, pad)), vm((ngrp, 8, pad)),
                 dma, dma, dma, dma,
-                dma((group,)), dma((group,)), dma, dma, dma, dma,
+                dma((group,)), dma((group,)), dma((group,)), dma((group,)), dma, dma((group,)), dma, dma, dma,
                 dma((4, 2)), dma((4, 2)),
-                dma, dma, dma, dma, dma, dma, dma, dma,
+                dma, dma, dma, dma, dma, dma, dma, dma, pltpu.SemaphoreType.REGULAR,
             ],
             compiler_params=pltpu.CompilerParams(
                 collective_id=0, has_side_effects=True, vmem_limit_bytes=48 * 1024 * 1024

time: 26.6 us -> 26 us (0.977)
  Pallas kernels: 25.9 us -> 25.2 us
    pallas_call x1, Pallas kernels: 25.1 us -> 24.4 us  [shards(): pl.pallas_call(functools.partial(kernel, ntier, ntile, nblk, group), out_...]
where the time goes in v3:
time: 26 us; the launch traced here: 25.8 us
  Pallas kernels  25.2 us (97%)
  between operations  0.64 us (2%)
    pallas_call x1, Pallas kernels, shards(): pl.pallas_call(functools.partial(kernel, ntier, ntile, nblk, group), out_...  24.4 us
    pallas_call x1, Pallas kernels, shards(): pl.pallas_call(last, out_shape=(jax.ShapeDtypeStruct(temp.shape, f32), ja...  0.8 us

profile of v3, /device:TPU:0, one launch (start us, length us, event | category | flops | bytes accessed | tf_op | source)
XLA Modules:
  0.0 25.8 jit_solution(16551108511442720746)
XLA Ops:
  0.6 24.4 %shard_map.86 = (f32[4,24,1024]{2,1,0:T(8,128)S(1)}, f32[1,16]{1,0:T(1,128)S(1)}, f32[24,1024]{1,0:T(8,128)S(1)}) custom-call(f32[4,24,1024]{2,1,0:T(8,128)} %t_hbm.1, s32[4,24,1024]{2,1,0:T(8,128)} %m_hbm.1, f32[2,8]{1,0:T(2,128)} %rates_hbm.1, s32[1,8]{1,0:T(1,128)} %labels_hbm.1, f32[4,16]{1,0:T(4,128)} %stat_hbm.1, f32[4,16]{1,0:T(4,128)} %fac_hbm.1, ...), custom_call_target="tpu_custom_call" | custom-call | tf_op jit(solution)/shard_map/pallas_call | solution.py:595
  25.0 0.8 %shard_map.87 = (f32[4,24,1024]{2,1,0:T(8,128)}, f32[1,16]{1,0:T(1,128)}) custom-call(f32[4,24,1024]{2,1,0:T(8,128)S(1)} %get-tuple-element.5.field, f32[24,1024]{1,0:T(8,128)S(1)} %get-tuple-element.6.lift, f32[1,16]{1,0:T(1,128)S(1)} %get-tuple-element.7.power), custom_call_target="tpu_custom_call" | custom-call | tf_op jit(solution)/shard_map/pallas_call | solution.py:619

commit v4 on v3

--- a/solution.py
+++ b/solution.py
@@ -38,11 +38,11 @@
     col_t, col_m, halo_t, halo_m, halo_1,
     pk_out, pk, halo_p,
     cx, cy, ce, mv, t1, t1c, res,
-    p1g, p1z, p2g, p2z,
+    p1g, p1z, p2,
     s_t, s_m, s_pk, s_o,
-    r_et, r_em, r_at, r_am, r_it, r_rt, r_rm, r_pk, r_o,
+    r_et, r_em, r_at, r_im, r_it, r_rt, r_rm, r_pk, r_o,
     s_h, r_h,
-    s_p1g, r_p1g, s_p1z, r_p1z, s_p2g, r_p2g, s_p2z, r_p2z, entered,
+    s_p1g, r_p1g, s_p1z, r_p1z, s_p2, r_p2, entered,
 ):
     tier = lax.axis_index("tier")
     tile = lax.axis_index("tile")
@@ -109,22 +109,18 @@
     for load in loads:
         load.wait()
 
-    sums = jnp.zeros((1, nblk), jnp.float32)
-    areas = jnp.zeros((1, nblk), jnp.float32)
-    names = jnp.zeros((1, C), jnp.float32)
+    note = lax.broadcasted_iota(jnp.int32, p1g.shape[1:], 1)
+    line = jnp.zeros(p1g.shape[1:], jnp.float32)
     active = t_in[0, 0:1, :]
     for r in range(1, rows):
         active = active + t_in[r, 0:1, :]
     for j in range(width // C):
+        label = labels[0, j]
         part = jnp.sum(active[:, j * C : (j + 1) * C], axis=1, keepdims=True)
-        hit = blk == labels[0, j]
-        sums = sums + jnp.where(hit, part, 0.0)
-        areas = areas + jnp.where(hit, float(rows * C), 0.0)
-        names = jnp.where(lane == j, labels[0, j].astype(jnp.float32), names)
-    p1g[own] = jnp.zeros(p1g.shape[1:], jnp.float32)
-    p1g[own, 0:1, 0:nblk] = sums
-    p1g[own, 1:2, 0:nblk] = areas
-    p1g[own, 2:3, 0:C] = names
+        line = line + jnp.where(note == label, part, 0.0)
+        line = line + jnp.where(note == nblk + label, float(rows * C), 0.0)
+        line = jnp.where(note == 2 * nblk + j, label.astype(jnp.float32), line)
+    p1g[own] = line
 
     pl.semaphore_wait(barrier, nwin - 1 + place)
     greet(entered, 0, place)
@@ -172,9 +168,8 @@
 
     edge = lax.select(sub == 0, 0, rows - 1)
     beside = lax.select(sub == 0, 1, rows - 2)
-    rest = lax.select(sub == 0, 2, 0)
+    other = lax.select(sub == 0, rows - 2, 1)
     inmost = lax.select(sub == 0, rows - 1, 0)
-    other = lax.select(sub == 0, rows - 2, 1)
     spread(t_hbm, col_t, edge, sub * rows + edge, 1, s_t, r_et.at[sub])
     spread(m_hbm, col_m, edge, sub * rows + edge, 1, s_m, r_em.at[sub])
 
@@ -200,6 +195,10 @@
                 whole = block if whole is None else whole + block
                 put = roll(block, 32 * g + 4 * r + 2)
                 second = put if second is None else jnp.where(quad == 8 * g + r, put, second)
+                put = roll(
+                    m_in[r, ls, w * C : (w + 1) * C].astype(jnp.float32), 32 * g + 4 * (rows + r) + 2
+                )
+                second = jnp.where(quad == 8 * g + rows + r, put, second)
             whole = jnp.sum(whole, axis=1, keepdims=True)
             second = jnp.where(lane == 32 * g + 3, whole, second)
         pk_out[w, 0] = first
@@ -214,10 +213,10 @@
                 src_ref=src_ref, dst_ref=dst_ref, send_sem=s_pk, recv_sem=r_pk,
                 device_id=there(t2, s2), device_id_type=MESH,
             ).start()
-    spread(m_hbm, col_m, beside, sub * rows + beside, 1, s_m, r_am.at[sub])
+    spread(m_hbm, col_m, inmost, sub * rows + inmost, 1, s_m, r_im)
+    spread(t_hbm, col_t, inmost, sub * rows + inmost, 1, s_t, r_it)
+    spread(m_hbm, col_m, 1, sub * rows + 1, rows - 2, s_m, r_rm.at[sub])
     spread(t_hbm, col_t, beside, sub * rows + beside, 1, s_t, r_at.at[sub])
-    spread(m_hbm, col_m, rest, sub * rows + rest, rows - 2, s_m, r_rm)
-    spread(t_hbm, col_t, inmost, sub * rows + inmost, 1, s_t, r_it)
     spread(t_hbm, col_t, other, sub * rows + other, 1, s_t, r_rt.at[sub])
 
     has_low = place > 0
@@ -256,20 +255,16 @@
 
     h_t = halo(col_t.at[0], col_t.at[grows - 1], halo_t, 0)
     h_m = halo(col_m.at[0], col_m.at[grows - 1], halo_m, 1)
-    h_p = halo(pk.at[0], pk.at[group - 1], halo_p, 2)
+    h_p = halo(pk.at[0, :, 0], pk.at[group - 1, :, 0], halo_p, 2)
     h_1 = halo(t1.at[0], t1.at[grows - 1], halo_1, 3)
 
     all_but_one(p1g, r_p1g)
     p1z[0] = jnp.zeros(p1z.shape[1:], jnp.float32)
     for t in range(ntier):
-        acc = p1g[t * group, 0:1, :]
+        acc = p1g[t * group]
         for s in range(1, group):
-            acc = acc + p1g[t * group + s, 0:1, :]
+            acc = acc + p1g[t * group + s]
         p1z[0, t : t + 1, :] = acc
-    acc = p1g[0, 1:2, :]
-    for s in range(1, group):
-        acc = acc + p1g[s, 1:2, :]
-    p1z[0, ntier : ntier + 1, :] = acc
     pl.when(has_high)(lambda: pl.semaphore_wait(entered, ngrp - 1 - place))
     across_send(p1z, s_p1z, r_p1z)
 
@@ -312,19 +307,45 @@
     out_t = unpack(lambda t: pk[0, t, 0], lambda t: pk[1, t, 0], 0, half, half)
     out_m = unpack(lambda t: pk[0, t, 0], lambda t: pk[1, t, 0], -half, 0, half)
     own_t = unpack(lambda t: pk[0, t, 1], lambda t: pk[1, t, 1], 0, half, half)
+    own_m = unpack(lambda t: pk[0, t, 1], lambda t: pk[1, t, 1], -half, 0, half)
     ixc, iyc = lookup(out_m, (0, 1))
+    (iyo,) = lookup(own_m, (1,))
     pos_low = (lane & 3) == 1
 
     op_active = [a_in[:, a : a + 1] for a in active_rows]
     op = jnp.concatenate(split(a_in[...]), axis=0)
 
+    there_is = jnp.where(pos_low, jnp.where(own > 0, 1.0, 0.0), jnp.where(own < nwin - 1, 1.0, 0.0))
+    c_in = there_is / (iyc + swap(iyo))
+    c_far = 1.0 / (iyc + jnp.where(pos_low, roll(iyc, 1), roll(iyc, -1)))
+    into_side = c_in * (swap(own_t) - out_t)
+    spun = swap(c_in)
+    kx = {}
+
+    def conduct(r):
+        kx[r], iy = lookup(col_m[r], (0, 1))
+        ce[r] = roll(spun, -(4 * r + 2))
+        cy[r] = jnp.where(lane == C - 1, ce[r], 1.0 / (iy + roll(iy, -1)))
+        for q in (r, r + 1):
+            if q - 1 in kx and q in kx:
+                cx[q] = 1.0 / (kx[q - 1] + kx[q])
+
+    outer = [0, grows - 1]
+    near = [1, grows - 2]
+    middle = list(range(2, grows - 2))
+    for r in outer:
+        conduct(r)
+    wait_for(col_m.at[pl.ds(rows - 1, 2)], r_im)
+    for r in (rows - 1, rows):
+        conduct(r)
+
     all_but_one(p1z, r_p1z)
     whole = total(p1z)
-    count = whole[ntier : ntier + 1, 0:nblk]
+    count = whole[0:1, nblk : 2 * nblk]
     power = stat[...] * jnp.exp(fac[...] * whole[0:ntier, 0:nblk] / count)
 
     def label_of(s, w):
-        return jnp.sum(jnp.where(lane == w, p1g[s, 2:3, 0:C], 0.0), axis=1, keepdims=True)
+        return jnp.sum(jnp.where(note == 2 * nblk + w, p1g[s], 0.0), axis=1, keepdims=True)
 
     blkf = blk.astype(jnp.float32)
 
@@ -348,46 +369,12 @@
     for t in range(1, ntier):
         lift_c = lift_c + op_active[t] * side[t : t + 1, :]
 
-    kx = {}
-    inner = {}
-    far = jnp.ones((levels, C), jnp.float32)
-
-    def conduct(r):
-        kx[r], iy = lookup(col_m[r], (0, 1))
-        cy[r] = 1.0 / (iy + roll(iy, -1))
-        inner[r] = roll(iy, 4 * r + 2)
-        for q in (r, r + 1):
-            if q - 1 in kx and q in kx:
-                cx[q] = 1.0 / (kx[q - 1] + kx[q])
-
-    there_is = jnp.where(pos_low, jnp.where(own > 0, 1.0, 0.0), jnp.where(own < nwin - 1, 1.0, 0.0))
-
-    def sideways(rs):
-        at = jnp.ones((levels, C), jnp.float32)
-        for r in rs:
-            at = jnp.where((lane >> 2) == r, inner[r], at)
-        c_in = there_is / (iyc + swap(at))
-        spun = swap(c_in)
-        for r in rs:
-            ce[r] = roll(spun, -(4 * r + 2))
-            cy[r] = jnp.where(lane == C - 1, ce[r], cy[r])
-        return c_in
-
-    c_far = 1.0 / (iyc + jnp.where(pos_low, roll(iyc, 1), roll(iyc, -1)))
-
-    outer = [0, grows - 1]
-    near = [1, grows - 2]
-    middle = list(range(2, grows - 2))
-    for s, row in ((0, 1), (group - 1, grows - 2)):
-        wait_for(col_m.at[row], r_am.at[s])
-    for r in outer + near:
-        conduct(r)
-    wait_for(col_m.at[pl.ds(2, grows - 4)], r_rm)
-    for r in middle:
-        conduct(r)
+    for s in range(group):
+        wait_for(col_m.at[pl.ds(s * rows + 1, rows - 2)], r_rm.at[s])
+    for s in range(group):
+        for r in range(s * rows + 1, (s + 1) * rows - 1):
+            conduct(r)
     first, last = kx[0], kx[grows - 1]
-    c_in = sideways(range(grows))
-    into_side = c_in * (swap(own_t) - out_t)
 
     halo_recv(h_m)
     halo_recv(h_p)
@@ -397,10 +384,10 @@
     cx[grows] = jnp.where(has_high, 1.0 / (ix + last), 0.0)
 
     end = 4 * (rows - 1)
-    up_t = unpack(lambda t: halo_p[0, t, 0], None, -end, 0, 0)
-    up_m = unpack(lambda t: halo_p[0, t, 0], None, -end - half, 0, 0)
-    dn_t = unpack(lambda t: halo_p[1, t, 0], None, 4 * (grows - 1), 0, 0)
-    dn_m = unpack(lambda t: halo_p[1, t, 0], None, 4 * (grows - 1) - half, 0, 0)
+    up_t = unpack(lambda t: halo_p[0, t], None, -end, 0, 0)
+    up_m = unpack(lambda t: halo_p[0, t], None, -end - half, 0, 0)
+    dn_t = unpack(lambda t: halo_p[1, t], None, 4 * (grows - 1), 0, 0)
+    dn_m = unpack(lambda t: halo_p[1, t], None, 4 * (grows - 1) - half, 0, 0)
     (up_ix,) = lookup(up_m, (0,))
     (dn_ix,) = lookup(dn_m, (0,))
     at_top = lane < 4
@@ -438,18 +425,6 @@
         above = halo_t[0] if r == 0 else col_t[r - 1]
         below = halo_t[1] if r == grows - 1 else col_t[r + 1]
         mv[:, at(r)] = lateral(col_t, spun, r, above, below)
-
-    for s, row in ((0, 1), (group - 1, grows - 2)):
-        wait_for(col_t.at[row], r_at.at[s])
-    for r in outer:
-        first_move(r)
-    mv[:, at(grows)] = part
-    both = solve(op, mv[:, at(0, 3)])
-    for i, r in enumerate(outer):
-        t1[r] = both[:, i * C : (i + 1) * C] + lift[r // rows]
-    t1c = both[:, 2 * C :] + lift_c
-    pl.when(has_low)(lambda: h_1[0].start())
-    pl.when(has_high)(lambda: h_1[1].start())
 
     wait_for(col_t.at[pl.ds(rows - 1, 2)], r_it)
     flows = [
@@ -473,16 +448,46 @@
         + [jnp.zeros((n_act - ntier, levels), jnp.float32)], axis=0
     )
     found = solve(jnp.concatenate(split(act), axis=0), jnp.concatenate(stock, axis=1))
-    p2g[own] = jnp.zeros(p2g.shape[1:], jnp.float32)
-    sums = jnp.zeros((ntier, nblk), jnp.float32)
+    slot = place * nwin + own
+    note2 = lax.broadcasted_iota(jnp.int32, p2.shape[1:], 1)
+    line = jnp.zeros(p2.shape[1:], jnp.float32)
     for s in range(group):
         acc = jnp.sum(found[0:ntier, s * C : (s + 1) * C], axis=1, keepdims=True)
         acc = acc + float(rows * C) * jnp.concatenate(
             [lift[s][a : a + 1, :] for a in active_rows], axis=0
         )
-        sums = sums + jnp.where(blkf == own_labels[s], acc, 0.0)
-    p2g[own, 0:ntier, 0:nblk] = sums
-    group_send(p2g, s_p2g, r_p2g)
+        name = own_labels[s].astype(jnp.int32)
+        for t in range(ntier):
+            line = line + jnp.where(note2 == t * nblk + name, acc[t : t + 1, :], 0.0)
+    p2[slot] = line
+
+    def to_all(t2, tile2):
+        pltpu.make_async_remote_copy(
+            src_ref=p2.at[slot], dst_ref=p2.at[slot], send_sem=s_p2, recv_sem=r_p2,
+            device_id={"tier": t2, "tile": tile2}, device_id_type=MESH,
+        ).start()
+
+    def to_group(k, carry):
+        for _, t2, s2 in peers:
+            to_all(t2, lax.rem(base + k * group, ntile) + s2)
+        return carry
+
+    lax.fori_loop(1, ngrp, to_group, 0)
+    for mine, t2, s2 in peers:
+        if not mine:
+            to_all(t2, base + s2)
+
+    for s, row in ((0, 1), (group - 1, grows - 2)):
+        wait_for(col_t.at[row], r_at.at[s])
+    for r in outer:
+        first_move(r)
+    mv[:, at(grows)] = part
+    both = solve(op, mv[:, at(0, 3)])
+    for i, r in enumerate(outer):
+        t1[r] = both[:, i * C : (i + 1) * C] + lift[r // rows]
+    t1c = both[:, 2 * C :] + lift_c
+    pl.when(has_low)(lambda: h_1[0].start())
+    pl.when(has_high)(lambda: h_1[1].start())
 
     for s, row in ((0, rows - 2), (group - 1, rows + 1)):
         wait_for(col_t.at[row], r_rt.at[s])
@@ -524,20 +529,14 @@
         finish(list(range(s * rows + (s == 0), (s + 1) * rows - (s == group - 1))))
         send_rows(s, int(s == 0), rows - 1)
 
-    all_but_one(p2g, r_p2g)
-    acc = p2g[0]
-    for k in range(1, nwin):
-        acc = acc + p2g[k]
-    p2z[0] = acc
-    across_send(p2z, s_p2z, r_p2z)
-
     halo_recv(h_1)
     finish(outer)
     for s, r in ((0, 0), (group - 1, grows - 1)):
         send_rows(s, r - s * rows, 1)
 
-    all_but_one(p2z, r_p2z)
-    whole = total(p2z)
+    all_but_one(p2, r_p2)
+    whole = jnp.sum(p2[...], axis=0)
+    whole = jnp.concatenate([whole[:, t * nblk : (t + 1) * nblk] for t in range(ntier)], axis=0)
     power = stat[...] * jnp.exp(fac[...] * whole[0:ntier, 0:nblk] / count)
     mine = lax.broadcasted_iota(jnp.int32, (ntier, nblk), 0) == tier
     pw_out[...] = jnp.sum(jnp.where(mine, power, 0.0), axis=0, keepdims=True)
@@ -560,8 +559,7 @@
     wait_for(pk_out.at[sent], s_pk)
     all_but_one(p1g, s_p1g)
     all_but_one(p1z, s_p1z)
-    all_but_one(p2g, s_p2g)
-    all_but_one(p2z, s_p2z)
+    all_but_one(p2, s_p2)
 
 
 def last(field, lift, power, out, power_out, done, sem):
@@ -582,7 +580,7 @@
     def shards(temp, mats, rates, labels, stat, fac, op):
         rows, lev, width = temp.shape
         nblk = stat.shape[1]
-        pad = -(-nblk // 128) * 128
+        pad = lambda n: -(-n // C) * C
         group = width // (ntier * C)
         levels, grows, ngrp, nwin = lev * ntier, rows * group, ntile // group, width // C
         f32, i32 = jnp.float32, jnp.int32
@@ -602,14 +600,15 @@
                 pltpu.SMEM(labels.shape, i32), vm(stat.shape), vm(fac.shape), vm(op.shape),
                 dma((7,)),
                 vm(block), vm(block, i32), vm((2, levels, C)), vm((2, levels, C), i32), vm((2, levels, C)),
-                vm((nwin, 2, 8, C)), vm((group, ntier, 2, 8, C)), vm((2, ntier, 2, 8, C)),
+                vm((nwin, 2, 8, C)), vm((group, ntier, 2, 8, C)), vm((2, ntier, 8, C)),
                 vm((grows + 1, levels, C)), vm(block), vm(block), vm((levels, (grows + 1) * C)),
                 vm(block), vm((levels, C)), vm(block),
-                vm((nwin, 8, pad)), vm((ngrp, 8, pad)), vm((nwin, 8, pad)), vm((ngrp, 8, pad)),
+                vm((nwin, 1, pad(2 * nblk + nwin))), vm((ngrp, 8, pad(2 * nblk + nwin))),
+                vm((ngrp * nwin, 1, pad(ntier * nblk))),
                 dma, dma, dma, dma,
-                dma((group,)), dma((group,)), dma((group,)), dma((group,)), dma, dma((group,)), dma, dma, dma,
+                dma((group,)), dma((group,)), dma((group,)), dma, dma, dma((group,)), dma((group,)), dma, dma,
                 dma((4, 2)), dma((4, 2)),
-                dma, dma, dma, dma, dma, dma, dma, dma, pltpu.SemaphoreType.REGULAR,
+                dma, dma, dma, dma, dma, dma, pltpu.SemaphoreType.REGULAR,
             ],
             compiler_params=pltpu.CompilerParams(
                 collective_id=0, has_side_effects=True, vmem_limit_bytes=48 * 1024 * 1024

time: 26 us -> 24.9 us (0.958)
  Pallas kernels: 25.2 us -> 24.1 us
    pallas_call x1, Pallas kernels: 24.4 us -> 23.3 us  [shards(): pl.pallas_call(functools.partial(kernel, ntier, ntile, nblk, group), out_...]
where the time goes in v4:
time: 24.9 us; the launch traced here: 24.7 us
  Pallas kernels  24.1 us (97%)
  between operations  0.64 us (3%)
    pallas_call x1, Pallas kernels, shards(): pl.pallas_call(functools.partial(kernel, ntier, ntile, nblk, group), out_...  23.3 us
    pallas_call x1, Pallas kernels, shards(): pl.pallas_call(last, out_shape=(jax.ShapeDtypeStruct(temp.shape, f32), ja...  0.8 us

profile of v4, /device:TPU:0, one launch (start us, length us, event | category | flops | bytes accessed | tf_op | source)
XLA Modules:
  0.0 24.7 jit_solution(7745089459862153200)
XLA Ops:
  0.6 23.3 %shard_map.86 = (f32[4,24,1024]{2,1,0:T(8,128)S(1)}, f32[1,16]{1,0:T(1,128)S(1)}, f32[24,1024]{1,0:T(8,128)S(1)}) custom-call(f32[4,24,1024]{2,1,0:T(8,128)} %t_hbm.1, s32[4,24,1024]{2,1,0:T(8,128)} %m_hbm.1, f32[2,8]{1,0:T(2,128)} %rates_hbm.1, s32[1,8]{1,0:T(1,128)} %labels_hbm.1, f32[4,16]{1,0:T(4,128)} %stat_hbm.1, f32[4,16]{1,0:T(4,128)} %fac_hbm.1, ...), custom_call_target="tpu_custom_call" | custom-call | tf_op jit(solution)/shard_map/pallas_call | solution.py:593
  23.9 0.8 %shard_map.87 = (f32[4,24,1024]{2,1,0:T(8,128)}, f32[1,16]{1,0:T(1,128)}) custom-call(f32[4,24,1024]{2,1,0:T(8,128)S(1)} %get-tuple-element.5.field, f32[24,1024]{1,0:T(8,128)S(1)} %get-tuple-element.6.lift, f32[1,16]{1,0:T(1,128)S(1)} %get-tuple-element.7.power), custom_call_target="tpu_custom_call" | custom-call | tf_op jit(solution)/shard_map/pallas_call | solution.py:618

commit v5 on v4

--- a/solution.py
+++ b/solution.py
@@ -40,7 +40,7 @@
     cx, cy, ce, mv, t1, t1c, res,
     p1g, p1z, p2,
     s_t, s_m, s_pk, s_o,
-    r_et, r_em, r_at, r_im, r_it, r_rt, r_rm, r_pk, r_o,
+    r_et, r_em, r_bt, r_bm, r_it, r_im, r_om, r_rt, r_pk, r_o,
     s_h, r_h,
     s_p1g, r_p1g, s_p1z, r_p1z, s_p2, r_p2, entered,
 ):
@@ -68,12 +68,13 @@
     for load in loads:
         load.start()
 
+    turned = tier + 1 - 2 * lax.rem(tier, 2)
     peers = []
-    for a in range(ntier):
-        for b in range(group):
-            t2 = lax.rem(tier + a, ntier)
-            s2 = lax.rem(sub + b, group)
-            peers.append((a == 0 and b == 0, t2, s2))
+    for b in range(group - 1, -1, -1):
+        for a in range(ntier - 2, -1, -2):
+            for start in (tier, turned):
+                mine = a == 0 and b == 0 and start is tier
+                peers.append((mine, lax.rem(start + a, ntier), lax.rem(sub + b, group)))
 
     def there(t2, s2):
         return {"tier": t2, "tile": base + s2}
@@ -213,10 +214,11 @@
                 src_ref=src_ref, dst_ref=dst_ref, send_sem=s_pk, recv_sem=r_pk,
                 device_id=there(t2, s2), device_id_type=MESH,
             ).start()
+    spread(m_hbm, col_m, beside, sub * rows + beside, 1, s_m, r_bm.at[sub])
+    spread(t_hbm, col_t, beside, sub * rows + beside, 1, s_t, r_bt.at[sub])
     spread(m_hbm, col_m, inmost, sub * rows + inmost, 1, s_m, r_im)
     spread(t_hbm, col_t, inmost, sub * rows + inmost, 1, s_t, r_it)
-    spread(m_hbm, col_m, 1, sub * rows + 1, rows - 2, s_m, r_rm.at[sub])
-    spread(t_hbm, col_t, beside, sub * rows + beside, 1, s_t, r_at.at[sub])
+    spread(m_hbm, col_m, other, sub * rows + other, 1, s_m, r_om.at[sub])
     spread(t_hbm, col_t, other, sub * rows + other, 1, s_t, r_rt.at[sub])
 
     has_low = place > 0
@@ -319,12 +321,12 @@
     c_in = there_is / (iyc + swap(iyo))
     c_far = 1.0 / (iyc + jnp.where(pos_low, roll(iyc, 1), roll(iyc, -1)))
     into_side = c_in * (swap(own_t) - out_t)
-    spun = swap(c_in)
+    spun_c = swap(c_in)
     kx = {}
 
     def conduct(r):
         kx[r], iy = lookup(col_m[r], (0, 1))
-        ce[r] = roll(spun, -(4 * r + 2))
+        ce[r] = roll(spun_c, -(4 * r + 2))
         cy[r] = jnp.where(lane == C - 1, ce[r], 1.0 / (iy + roll(iy, -1)))
         for q in (r, r + 1):
             if q - 1 in kx and q in kx:
@@ -334,6 +336,9 @@
     near = [1, grows - 2]
     middle = list(range(2, grows - 2))
     for r in outer:
+        conduct(r)
+    for s, r in ((0, 1), (group - 1, grows - 2)):
+        wait_for(col_m.at[r], r_bm.at[s])
         conduct(r)
     wait_for(col_m.at[pl.ds(rows - 1, 2)], r_im)
     for r in (rows - 1, rows):
@@ -369,11 +374,6 @@
     for t in range(1, ntier):
         lift_c = lift_c + op_active[t] * side[t : t + 1, :]
 
-    for s in range(group):
-        wait_for(col_m.at[pl.ds(s * rows + 1, rows - 2)], r_rm.at[s])
-    for s in range(group):
-        for r in range(s * rows + 1, (s + 1) * rows - 1):
-            conduct(r)
     first, last = kx[0], kx[grows - 1]
 
     halo_recv(h_m)
@@ -416,7 +416,7 @@
 
     halo_recv(h_t)
     spun = swap(out_t)
-    place_of = {r: i for i, r in enumerate(outer + [grows] + list(range(1, grows - 1)))}
+    place_of = {r: i for i, r in enumerate(outer + [grows] + near + middle)}
 
     def at(r, n=1):
         return slice(place_of[r] * C, (place_of[r] + n) * C)
@@ -425,6 +425,18 @@
         above = halo_t[0] if r == 0 else col_t[r - 1]
         below = halo_t[1] if r == grows - 1 else col_t[r + 1]
         mv[:, at(r)] = lateral(col_t, spun, r, above, below)
+
+    for s, r in ((0, 1), (group - 1, grows - 2)):
+        wait_for(col_t.at[r], r_bt.at[s])
+    for r in outer:
+        first_move(r)
+    mv[:, at(grows)] = part
+    both = solve(op, mv[:, at(0, 3)])
+    for i, r in enumerate(outer):
+        t1[r] = both[:, i * C : (i + 1) * C] + lift[r // rows]
+    t1c = both[:, 2 * C :] + lift_c
+    pl.when(has_low)(lambda: h_1[0].start())
+    pl.when(has_high)(lambda: h_1[1].start())
 
     wait_for(col_t.at[pl.ds(rows - 1, 2)], r_it)
     flows = [
@@ -477,42 +489,34 @@
         if not mine:
             to_all(t2, base + s2)
 
-    for s, row in ((0, 1), (group - 1, grows - 2)):
-        wait_for(col_t.at[row], r_at.at[s])
-    for r in outer:
-        first_move(r)
-    mv[:, at(grows)] = part
-    both = solve(op, mv[:, at(0, 3)])
-    for i, r in enumerate(outer):
-        t1[r] = both[:, i * C : (i + 1) * C] + lift[r // rows]
-    t1c = both[:, 2 * C :] + lift_c
-    pl.when(has_low)(lambda: h_1[0].start())
-    pl.when(has_high)(lambda: h_1[1].start())
+    for s, r in ((0, rows - 2), (group - 1, rows + 1)):
+        wait_for(col_m.at[r], r_om.at[s])
+        conduct(r)
 
     for s, row in ((0, rows - 2), (group - 1, rows + 1)):
         wait_for(col_t.at[row], r_rt.at[s])
     for r in near + middle:
         first_move(r)
     most = solve(op, mv[:, at(1, grows - 2)])
-    for r in range(1, grows - 1):
-        t1[r] = most[:, (r - 1) * C : r * C] + lift[r // rows]
-
-    def send_rows(s, first_row, count):
-        for t in range(ntier):
-            for_me = jnp.logical_and(tier == t, sub == s)
-            src_ref = res.at[pl.ds(s * rows + first_row, count), pl.ds(t * lev, lev), :]
-            dst_ref = out.at[pl.ds(first_row, count), :, cols(own)]
-
-            @pl.when(for_me)
-            def _():
-                pltpu.make_async_copy(src_ref, dst_ref, r_o).start()
-
-            @pl.when(jnp.logical_not(for_me))
-            def _():
-                pltpu.make_async_remote_copy(
-                    src_ref=src_ref, dst_ref=dst_ref, send_sem=s_o, recv_sem=r_o,
-                    device_id=there(t, s), device_id_type=MESH,
-                ).start()
+    for i, r in enumerate(near + middle):
+        t1[r] = most[:, i * C : (i + 1) * C] + lift[r // rows]
+
+    own_tile, next_tile = peers[-ntier:], peers[:-ntier]
+
+    def send_rows(first_low, first_high, count):
+        to_own = lax.select(sub == 0, first_low, first_high)
+        to_next = lax.select(sub == 0, first_high, first_low)
+        for whom, row in ((next_tile, to_next), (own_tile, to_own)):
+            for mine, t2, s2 in whom:
+                src_ref = res.at[pl.ds(row, count), levs(t2), :]
+                dst_ref = out.at[pl.ds(row - s2 * rows, count), :, cols(own)]
+                if mine:
+                    pltpu.make_async_copy(src_ref, dst_ref, r_o).start()
+                else:
+                    pltpu.make_async_remote_copy(
+                        src_ref=src_ref, dst_ref=dst_ref, send_sem=s_o, recv_sem=r_o,
+                        device_id=there(t2, s2), device_id_type=MESH,
+                    ).start()
 
     spun = swap(t1c)
 
@@ -525,14 +529,12 @@
         for i, r in enumerate(rs):
             res[r] = x[:, i * C : (i + 1) * C]
 
-    for s in range(group):
-        finish(list(range(s * rows + (s == 0), (s + 1) * rows - (s == group - 1))))
-        send_rows(s, int(s == 0), rows - 1)
-
+    finish(middle)
+    send_rows(2, rows, rows - 2)
+    finish(near)
     halo_recv(h_1)
     finish(outer)
-    for s, r in ((0, 0), (group - 1, grows - 1)):
-        send_rows(s, r - s * rows, 1)
+    send_rows(0, grows - 2, 2)
 
     all_but_one(p2, r_p2)
     whole = jnp.sum(p2[...], axis=0)
@@ -594,7 +596,7 @@
             functools.partial(kernel, ntier, ntile, nblk, group),
             out_shape=(vm(temp.shape), vm((1, nblk)), vm((lev, width))),
             in_specs=[pl.BlockSpec(memory_space=pltpu.HBM)] * 7,
-            out_specs=(vmem, vmem, vmem),
+            out_specs=(pl.BlockSpec(memory_space=pl.ANY), vmem, vmem),
             scratch_shapes=[
                 vm(temp.shape), vm(mats.shape, i32), vm(rates.shape),
                 pltpu.SMEM(labels.shape, i32), vm(stat.shape), vm(fac.shape), vm(op.shape),
@@ -606,7 +608,8 @@
                 vm((nwin, 1, pad(2 * nblk + nwin))), vm((ngrp, 8, pad(2 * nblk + nwin))),
                 vm((ngrp * nwin, 1, pad(ntier * nblk))),
                 dma, dma, dma, dma,
-                dma((group,)), dma((group,)), dma((group,)), dma, dma, dma((group,)), dma((group,)), dma, dma,
+                dma((group,)), dma((group,)), dma((group,)), dma((group,)), dma, dma, dma((group,)),
+                dma((group,)), dma, dma,
                 dma((4, 2)), dma((4, 2)),
                 dma, dma, dma, dma, dma, dma, pltpu.SemaphoreType.REGULAR,
             ],

time: 24.9 us -> 24.5 us (0.984)
  Pallas kernels: 24.1 us -> 23.7 us
    pallas_call x1, Pallas kernels: 23.3 us -> 22.9 us  [shards(): pl.pallas_call(functools.partial(kernel, ntier, ntile, nblk, group), out_...]
where the time goes in v5:
time: 24.5 us; the launch traced here: 24.3 us
  Pallas kernels  23.7 us (97%)
  between operations  0.64 us (3%)
    pallas_call x1, Pallas kernels, shards(): pl.pallas_call(functools.partial(kernel, ntier, ntile, nblk, group), out_...  22.9 us
    pallas_call x1, Pallas kernels, shards(): pl.pallas_call(last, out_shape=(jax.ShapeDtypeStruct(temp.shape, f32), ja...  0.8 us

profile of v5, /device:TPU:0, one launch (start us, length us, event | category | flops | bytes accessed | tf_op | source)
XLA Modules:
  0.0 24.3 jit_solution(3659066520946451326)
XLA Ops:
  0.6 22.9 %shard_map.86 = (f32[4,24,1024]{2,1,0:T(8,128)S(1)}, f32[1,16]{1,0:T(1,128)S(1)}, f32[24,1024]{1,0:T(8,128)S(1)}) custom-call(f32[4,24,1024]{2,1,0:T(8,128)} %t_hbm.1, s32[4,24,1024]{2,1,0:T(8,128)} %m_hbm.1, f32[2,8]{1,0:T(2,128)} %rates_hbm.1, s32[1,8]{1,0:T(1,128)} %labels_hbm.1, f32[4,16]{1,0:T(4,128)} %stat_hbm.1, f32[4,16]{1,0:T(4,128)} %fac_hbm.1, ...), custom_call_target="tpu_custom_call" | custom-call | tf_op jit(solution)/shard_map/pallas_call | solution.py:595
  23.5 0.8 %shard_map.87 = (f32[4,24,1024]{2,1,0:T(8,128)}, f32[1,16]{1,0:T(1,128)}) custom-call(f32[4,24,1024]{2,1,0:T(8,128)S(1)} %get-tuple-element.5.field, f32[24,1024]{1,0:T(8,128)S(1)} %get-tuple-element.6.lift, f32[1,16]{1,0:T(1,128)S(1)} %get-tuple-element.7.power), custom_call_target="tpu_custom_call" | custom-call | tf_op jit(solution)/shard_map/pallas_call | solution.py:621

commit v6 on v5

--- a/solution.py
+++ b/solution.py
@@ -376,13 +376,44 @@
 
     first, last = kx[0], kx[grows - 1]
 
+    def lateral(field, outside, r, above, below):
+        here = field[r]
+        edge_in = roll(outside, -(4 * r + 2))
+        beside = jnp.where(lane == C - 1, edge_in, roll(here, -1))
+        flux = cy[r] * (beside - here)
+        left = jnp.where(lane == 0, ce[r] * (here - edge_in), roll(flux, 1))
+        moved = here + (flux - left)
+        return moved + cx[r + 1] * (below - here) - cx[r] * (here - above)
+
     halo_recv(h_m)
-    halo_recv(h_p)
     (ix,) = lookup(halo_m[0], (0,))
     cx[0] = jnp.where(has_low, 1.0 / (ix + first), 0.0)
     (ix,) = lookup(halo_m[1], (0,))
     cx[grows] = jnp.where(has_high, 1.0 / (ix + last), 0.0)
 
+    halo_recv(h_t)
+    spun = swap(out_t)
+    place_of = {r: i for i, r in enumerate(outer + [grows] + near + middle)}
+
+    def at(r, n=1):
+        return slice(place_of[r] * C, (place_of[r] + n) * C)
+
+    def first_move(r):
+        above = halo_t[0] if r == 0 else col_t[r - 1]
+        below = halo_t[1] if r == grows - 1 else col_t[r + 1]
+        mv[:, at(r)] = lateral(col_t, spun, r, above, below)
+
+    for s, r in ((0, 1), (group - 1, grows - 2)):
+        wait_for(col_t.at[r], r_bt.at[s])
+    for r in outer:
+        first_move(r)
+    both = solve(op, mv[:, at(0, 2)])
+    for i, r in enumerate(outer):
+        t1[r] = both[:, i * C : (i + 1) * C] + lift[r // rows]
+    pl.when(has_low)(lambda: h_1[0].start())
+    pl.when(has_high)(lambda: h_1[1].start())
+
+    halo_recv(h_p)
     end = 4 * (rows - 1)
     up_t = unpack(lambda t: halo_p[0, t], None, -end, 0, 0)
     up_m = unpack(lambda t: halo_p[0, t], None, -end - half, 0, 0)
@@ -405,38 +436,8 @@
     )
 
 
-    def lateral(field, outside, r, above, below):
-        here = field[r]
-        edge_in = roll(outside, -(4 * r + 2))
-        beside = jnp.where(lane == C - 1, edge_in, roll(here, -1))
-        flux = cy[r] * (beside - here)
-        left = jnp.where(lane == 0, ce[r] * (here - edge_in), roll(flux, 1))
-        moved = here + (flux - left)
-        return moved + cx[r + 1] * (below - here) - cx[r] * (here - above)
-
-    halo_recv(h_t)
-    spun = swap(out_t)
-    place_of = {r: i for i, r in enumerate(outer + [grows] + near + middle)}
-
-    def at(r, n=1):
-        return slice(place_of[r] * C, (place_of[r] + n) * C)
-
-    def first_move(r):
-        above = halo_t[0] if r == 0 else col_t[r - 1]
-        below = halo_t[1] if r == grows - 1 else col_t[r + 1]
-        mv[:, at(r)] = lateral(col_t, spun, r, above, below)
-
-    for s, r in ((0, 1), (group - 1, grows - 2)):
-        wait_for(col_t.at[r], r_bt.at[s])
-    for r in outer:
-        first_move(r)
     mv[:, at(grows)] = part
-    both = solve(op, mv[:, at(0, 3)])
-    for i, r in enumerate(outer):
-        t1[r] = both[:, i * C : (i + 1) * C] + lift[r // rows]
-    t1c = both[:, 2 * C :] + lift_c
-    pl.when(has_low)(lambda: h_1[0].start())
-    pl.when(has_high)(lambda: h_1[1].start())
+
 
     wait_for(col_t.at[pl.ds(rows - 1, 2)], r_it)
     flows = [
@@ -497,9 +498,10 @@
         wait_for(col_t.at[row], r_rt.at[s])
     for r in near + middle:
         first_move(r)
-    most = solve(op, mv[:, at(1, grows - 2)])
+    most = solve(op, mv[:, at(grows, grows - 1)])
     for i, r in enumerate(near + middle):
-        t1[r] = most[:, i * C : (i + 1) * C] + lift[r // rows]
+        t1[r] = most[:, (i + 1) * C : (i + 2) * C] + lift[r // rows]
+    t1c = most[:, :C] + lift_c
 
     own_tile, next_tile = peers[-ntier:], peers[:-ntier]
 

time: 24.5 us -> 24.3 us (level)
  no operation moved by 1% of the time
where the time goes in v6:
time: 24.3 us; the launch traced here: 24.2 us
  Pallas kernels  23.5 us (97%)
  between operations  0.64 us (3%)
    pallas_call x1, Pallas kernels, shards(): pl.pallas_call(functools.partial(kernel, ntier, ntile, nblk, group), out_...  22.7 us
    pallas_call x1, Pallas kernels, shards(): pl.pallas_call(last, out_shape=(jax.ShapeDtypeStruct(temp.shape, f32), ja...  0.8 us

profile of v6, /device:TPU:0, one launch (start us, length us, event | category | flops | bytes accessed | tf_op | source)
XLA Modules:
  0.0 24.2 jit_solution(3662435677416793440)
XLA Ops:
  0.6 22.7 %shard_map.86 = (f32[4,24,1024]{2,1,0:T(8,128)S(1)}, f32[1,16]{1,0:T(1,128)S(1)}, f32[24,1024]{1,0:T(8,128)S(1)}) custom-call(f32[4,24,1024]{2,1,0:T(8,128)} %t_hbm.1, s32[4,24,1024]{2,1,0:T(8,128)} %m_hbm.1, f32[2,8]{1,0:T(2,128)} %rates_hbm.1, s32[1,8]{1,0:T(1,128)} %labels_hbm.1, f32[4,16]{1,0:T(4,128)} %stat_hbm.1, f32[4,16]{1,0:T(4,128)} %fac_hbm.1, ...), custom_call_target="tpu_custom_call" | custom-call | tf_op jit(solution)/shard_map/pallas_call | solution.py:597
  23.4 0.8 %shard_map.87 = (f32[4,24,1024]{2,1,0:T(8,128)}, f32[1,16]{1,0:T(1,128)}) custom-call(f32[4,24,1024]{2,1,0:T(8,128)S(1)} %get-tuple-element.5.field, f32[24,1024]{1,0:T(8,128)S(1)} %get-tuple-element.6.lift, f32[1,16]{1,0:T(1,128)S(1)} %get-tuple-element.7.power), custom_call_target="tpu_custom_call" | custom-call | tf_op jit(solution)/shard_map/pallas_call | solution.py:623

commit v7 on v6

--- a/solution.py
+++ b/solution.py
@@ -250,10 +250,6 @@
     def halo_recv(copies):
         pl.when(has_low)(lambda: copies[1].wait_recv())
         pl.when(has_high)(lambda: copies[0].wait_recv())
-
-    def halo_sent(copies):
-        pl.when(has_low)(lambda: copies[0].wait_send())
-        pl.when(has_high)(lambda: copies[1].wait_send())
 
     h_t = halo(col_t.at[0], col_t.at[grows - 1], halo_t, 0)
     h_m = halo(col_m.at[0], col_m.at[grows - 1], halo_m, 1)
@@ -552,18 +548,22 @@
             a = active_rows[t]
             acc = acc + own_op[:, a : a + 1] * g[t : t + 1, :]
         lift_out[:, j * C : (j + 1) * C] = jnp.broadcast_to(acc, (lev, C))
-    wait_for(out, r_o)
-
-    for copies in (h_t, h_m, h_p, h_1):
-        halo_sent(copies)
+
+    def passed(side):
+        for copies in (h_t, h_m, h_p, h_1):
+            copies[side].wait_send()
+
+    pl.when(has_low)(lambda: passed(0))
+    pl.when(has_high)(lambda: passed(1))
     sent = pl.ds(0, nwin - 1)
     wait_for(res.at[sent], s_t)
     wait_for(res.at[sent], s_m)
-    wait_for(res.at[sent], s_o)
     wait_for(pk_out.at[sent], s_pk)
     all_but_one(p1g, s_p1g)
     all_but_one(p1z, s_p1z)
     all_but_one(p2, s_p2)
+    wait_for(res.at[sent], s_o)
+    wait_for(out, r_o)
 
 
 def last(field, lift, power, out, power_out, done, sem):

time: 24.3 us -> 24.3 us (level)
  no operation moved by 1% of the time
where the time goes in v7:
time: 24.3 us; the launch traced here: 24.2 us
  Pallas kernels  23.5 us (97%)
  between operations  0.64 us (3%)
    pallas_call x1, Pallas kernels, shards(): pl.pallas_call(functools.partial(kernel, ntier, ntile, nblk, group), out_...  22.7 us
    pallas_call x1, Pallas kernels, shards(): pl.pallas_call(last, out_shape=(jax.ShapeDtypeStruct(temp.shape, f32), ja...  0.8 us

profile of v7, /device:TPU:0, one launch (start us, length us, event | category | flops | bytes accessed | tf_op | source)
XLA Modules:
  0.0 24.2 jit_solution(11088241587120649232)
XLA Ops:
  0.6 22.7 %shard_map.86 = (f32[4,24,1024]{2,1,0:T(8,128)S(1)}, f32[1,16]{1,0:T(1,128)S(1)}, f32[24,1024]{1,0:T(8,128)S(1)}) custom-call(f32[4,24,1024]{2,1,0:T(8,128)} %t_hbm.1, s32[4,24,1024]{2,1,0:T(8,128)} %m_hbm.1, f32[2,8]{1,0:T(2,128)} %rates_hbm.1, s32[1,8]{1,0:T(1,128)} %labels_hbm.1, f32[4,16]{1,0:T(4,128)} %stat_hbm.1, f32[4,16]{1,0:T(4,128)} %fac_hbm.1, ...), custom_call_target="tpu_custom_call" | custom-call | tf_op jit(solution)/shard_map/pallas_call | solution.py:597
  23.4 0.8 %shard_map.87 = (f32[4,24,1024]{2,1,0:T(8,128)}, f32[1,16]{1,0:T(1,128)}) custom-call(f32[4,24,1024]{2,1,0:T(8,128)S(1)} %get-tuple-element.5.field, f32[24,1024]{1,0:T(8,128)S(1)} %get-tuple-element.6.lift, f32[1,16]{1,0:T(1,128)S(1)} %get-tuple-element.7.power), custom_call_target="tpu_custom_call" | custom-call | tf_op jit(solution)/shard_map/pallas_call | solution.py:623
